TPU v7x, 32 devices: a whole 2x2x4 slice. The times are simulated.
32 devices in a mesh: ctx: 16 (over z, x, core), head: 2 (over y).
Axes of the slice: x: 2, y: 2, z: 4, core: 2. Of those that a mesh axis runs over, the one named last changes fastest.
Arguments:
- queries: bfloat16 [2048, 1024], P('ctx', 'head'), may hold values from -80 to 80
- keys: bfloat16 [2048, 256], P('ctx', 'head'), may hold values from -80 to 80
- values: bfloat16 [2048, 256], P('ctx', 'head'), may hold values from -6 to 6
- feat_q: bfloat16 [8, 128, 64], P('head'), may hold values from -1 to 1
- feat_k: bfloat16 [8, 128, 64], P('head'), may hold values from -1 to 1
Outputs:
- student: bfloat16 [2048, 1024], P('ctx', 'head')
- grad_q: float32 [8, 128, 64], P('head')
- grad_k: float32 [8, 128, 64], P('head')
- mean_error: float32 [], replicated
All inputs are finite; a program needn't handle non-finite values.
Results may differ from a plain program's by a relative error of at most 0.007.
The roundings to bfloat16 on the way count: a program that leaves them out, or rounds other values in their place, can miss the bound.
Values may be sent and summed in bfloat16 or wider, within the bound.
A program may use at most 128 MiB of HBM per device.

v0:
```python
import jax
import jax.numpy as jnp
from jax import lax
from jax.sharding import PartitionSpec as P

precise_scores = lax.Precision.HIGHEST


def entering(value, axis, combine, identity):
    length, here = (lax.axis_size(axis), lax.axis_index(axis))
    everything = jax.tree.map(
        lambda part, kind: lax.all_gather(part.astype(kind), axis),
        value,
        (jnp.bfloat16, jnp.bfloat16),
    )
    start = jax.tree.map(
        lambda part, zero: jnp.broadcast_to(jnp.asarray(zero, part.dtype), part.shape),
        value,
        identity,
    )

    def turn(k, before):
        at = length - 1 - k
        reached = at > here
        new = combine(
            before, jax.tree.map(lambda part, own: part[at].astype(own.dtype), everything, value)
        )
        return jax.tree.map(lambda a, b: jnp.where(reached, a, b), new, before)

    return lax.fori_loop(0, length, turn, start)


def feature_map(logits):
    positive = jax.nn.softmax(logits, axis=-1)
    negative = jax.nn.softmax(-logits, axis=-1)
    return (positive, negative, jnp.concatenate([positive, negative], axis=-1).astype(jnp.bfloat16))


def feature_grad(positive, negative, upstream):
    width = positive.shape[-1]
    up_pos = upstream[..., :width]
    up_neg = upstream[..., width:]
    return positive * (up_pos - jnp.sum(up_pos * positive, axis=-1, keepdims=True)) - negative * (
        up_neg - jnp.sum(up_neg * negative, axis=-1, keepdims=True)
    )


def masked_update(partial_value_sum, score_matrix, query_pos, value_piece):
    running, totals, accumulated_output = partial_value_sum
    key_positions = jnp.arange(value_piece.shape[0], dtype=jnp.int32)
    allowed = (query_pos[:, None] >= key_positions[None, :])[:, None, :]
    score_matrix = jnp.where(allowed, score_matrix, -1e30)
    new_max = jnp.maximum(running, jnp.max(score_matrix, axis=-1))
    attention_weights = jnp.where(allowed, jnp.exp(score_matrix - new_max[..., None]), 0.0)
    totals = jnp.sum(attention_weights, axis=-1)
    accumulated_output = jnp.einsum(
        "rgk,kd->rgd",
        attention_weights.astype(jnp.bfloat16),
        value_piece,
        preferred_element_type=jnp.float32,
    )
    return (new_max, totals, accumulated_output)


def plain_update(partial_value_sum, score_matrix, value_piece):
    running, totals, accumulated_output = partial_value_sum
    new_max = jnp.maximum(running, jnp.max(score_matrix, axis=-1))
    attention_weights = jnp.exp(score_matrix - new_max[..., None])
    totals = jnp.sum(attention_weights, axis=-1)
    accumulated_output = jnp.einsum(
        "rgk,kd->rgd",
        attention_weights.astype(jnp.bfloat16),
        value_piece,
        preferred_element_type=jnp.float32,
    )
    return (new_max, totals, accumulated_output)


def attend(partial_value_sum, query_rows, query_pos, key_piece, value_piece, offset, logit_scale):
    score_matrix = (
        jnp.einsum("rgd,kd->rgk", query_rows, key_piece, preferred_element_type=jnp.float32)
        * logit_scale
    )
    needs_mask = offset + key_piece.shape[0] - 1 > jnp.min(query_pos)
    return lax.cond(
        needs_mask,
        lambda scores: masked_update(partial_value_sum, scores, query_pos, value_piece),
        lambda scores: plain_update(partial_value_sum, scores, value_piece),
        score_matrix,
    )


def add_pair(earlier, later):
    return (earlier[0] + later[0], earlier[1] + later[1])


def on_device(queries, keys, values, feat_q, feat_k):
    row_count = queries.shape[0]
    group_size = feat_q.shape[0]
    head_dim = keys.shape[1]
    feature_dim = feat_q.shape[2]
    ctx_count = lax.axis_size("ctx")
    ctx_index = lax.axis_index("ctx")
    logit_scale = head_dim ** (-0.5)
    query_heads = queries.reshape(row_count, group_size, head_dim)
    first_row = ctx_index * row_count
    teacher_pos = first_row + jnp.arange(row_count, dtype=jnp.int32)
    initial = (
        jnp.full((row_count, group_size), -1e30, jnp.float32),
        jnp.zeros((row_count, group_size), jnp.float32),
        jnp.zeros((row_count, group_size, head_dim), jnp.float32),
    )
    pieces = (
        lax.all_gather(keys, "ctx", axis=0, tiled=True),
        lax.all_gather(values, "ctx", axis=0, tiled=True),
    )
    offset = jnp.int32(0)
    running, totals, accumulated_output = lax.cond(
        offset < first_row + row_count,
        lambda inner: attend(
            inner, query_heads, teacher_pos, pieces[0], pieces[1], offset, logit_scale
        ),
        lambda inner: inner,
        initial,
    )
    teacher = accumulated_output / totals[..., None]
    pos_q, neg_q, feat_query = feature_map(
        jnp.einsum("rgd,gdf->rgf", query_heads, feat_q, preferred_element_type=jnp.float32)
    )
    pos_k, neg_k, feat_key = feature_map(
        jnp.einsum("rd,gdf->rgf", keys, feat_k, preferred_element_type=jnp.float32)
    )
    zero_state = (
        jnp.zeros((group_size, 2 * feature_dim, head_dim), jnp.float32),
        jnp.zeros((group_size, 2 * feature_dim), jnp.float32),
    )
    state_pieces = (
        lax.all_gather(keys, "ctx", axis=0, tiled=True),
        lax.all_gather(values, "ctx", axis=0, tiled=True),
    )

    def absorb_block(inner):
        pos_piece, neg_piece, piece_feat = feature_map(
            jnp.einsum("rd,gdf->rgf", state_pieces[0], feat_k, preferred_element_type=jnp.float32)
        )
        key_positions = jnp.arange(state_pieces[0].shape[0], dtype=jnp.int32)
        piece_feat = jnp.where(
            (key_positions < first_row)[:, None, None], piece_feat, jnp.zeros_like(piece_feat)
        )
        return (
            jnp.einsum(
                "jgf,jd->gfd", piece_feat, state_pieces[1], preferred_element_type=jnp.float32
            ),
            jnp.sum(piece_feat.astype(jnp.float32), axis=0),
        )

    prior_state, prior_norm = lax.cond(
        jnp.int32(0) < first_row, absorb_block, lambda inner: inner, zero_state
    )
    positions = jnp.arange(row_count, dtype=jnp.int32)
    causal = positions[:, None] >= positions[None, :]
    amat = jnp.einsum("igf,jgf->gij", feat_query, feat_key, preferred_element_type=jnp.float32)
    amat = jnp.where(causal[None], amat, 0.0)
    feat_q32 = feat_query.astype(jnp.float32)
    numer = jnp.einsum(
        "gij,jd->igd", amat.astype(jnp.bfloat16), values, preferred_element_type=jnp.float32
    ) + jnp.einsum("igf,gfd->igd", feat_q32, prior_state, precision=precise_scores)
    denom = jnp.sum(amat, axis=-1).T + jnp.einsum(
        "igf,gf->ig", feat_q32, prior_norm, precision=precise_scores
    )
    student = numer / denom[..., None]
    diff = student - teacher
    error_local = jnp.sum(diff * diff)
    grad_out = 2.0 * diff
    grad_numer = grad_out / denom[..., None]
    grad_denom = -jnp.sum(grad_out * student, axis=-1) / denom
    numer_bf = grad_numer.astype(jnp.bfloat16)
    grad_mat = (
        jnp.einsum("igd,jd->gij", numer_bf, values, preferred_element_type=jnp.float32)
        + grad_denom.T[:, :, None]
    )
    grad_mat = jnp.where(causal[None], grad_mat, 0.0).astype(jnp.bfloat16)
    grad_fq = (
        jnp.einsum("gij,jgf->igf", grad_mat, feat_key, preferred_element_type=jnp.float32)
        + jnp.einsum("igd,gfd->igf", grad_numer, prior_state, precision=precise_scores)
        + grad_denom[..., None] * prior_norm[None]
    )
    local_grad_state = jnp.einsum(
        "igf,igd->gfd", feat_query, numer_bf, preferred_element_type=jnp.float32
    )
    local_grad_norm = jnp.einsum("igf,ig->gf", feat_q32, grad_denom, precision=precise_scores)
    later_state, later_norm = entering(
        (local_grad_state, local_grad_norm), "ctx", add_pair, zero_state
    )
    grad_fk = (
        jnp.einsum("gij,igf->jgf", grad_mat, feat_query, preferred_element_type=jnp.float32)
        + jnp.einsum(
            "gfd,jd->jgf", later_state, values.astype(jnp.float32), precision=precise_scores
        )
        + later_norm[None]
    )
    grad_logit_q = feature_grad(pos_q, neg_q, grad_fq).astype(jnp.bfloat16)
    grad_logit_k = feature_grad(pos_k, neg_k, grad_fk).astype(jnp.bfloat16)
    weight_q = jnp.einsum(
        "rgd,rgf->gdf", query_heads, grad_logit_q, preferred_element_type=jnp.float32
    )
    weight_k = jnp.einsum("rd,rgf->gdf", keys, grad_logit_k, preferred_element_type=jnp.float32)
    grad_query, grad_key = lax.psum((weight_q, weight_k), "ctx")
    error_all = lax.psum(error_local, ("ctx", "head"))
    entry_count = ctx_count * row_count * group_size * lax.axis_size("head") * head_dim
    mean_error = error_all / entry_count
    return (
        student.reshape(row_count, group_size * head_dim).astype(jnp.bfloat16),
        grad_query,
        grad_key,
        mean_error,
    )


def solution(mesh):
    in_specs = (
        P("ctx", "head"),
        P("ctx", "head"),
        P("ctx", "head"),
        P("head", None, None),
        P("head", None, None),
    )
    out_specs = (P("ctx", "head"), P("head", None, None), P("head", None, None), P())
    return jax.shard_map(
        on_device, mesh=mesh, in_specs=in_specs, out_specs=out_specs, check_vma=False
    )
```

profile of v0, /device:TPU:0, one launch (start us, length us, event | category | flops | bytes accessed | tf_op | source)
XLA Modules:
  0.0 245.9 jit_solution(3296679325642088650)
XLA Ops:
  7.2 0.0 all-gather.5.cloned.1.call-start
  7.2 1.0 copy.43
  8.3 1.4 fusion.100
  9.7 1.4 fusion.101
  11.1 24.8 %all_gather.20 = bf16[2048,128]{1,0:T(8,128)(2,1)S(1)} all-gather(bf16[128,128]{1,0:T(8,128)(2,1)} %param.14), channel_id=1, replica_groups=mesh['ctx'=16,'head'=2] {'ctx'}, dimensions={0}, use_global_device_ids=true | all-gather | bytes 557056 | tf_op jit(solution)/shard_map/all_gather | solution.py:138
  35.9 1.0 fusion.104
  36.9 0.8 fusion.98
  37.7 1.3 fusion.99
  39.0 19.1 %all_gather.21 = bf16[2048,128]{1,0:T(8,128)(2,1)S(1)} all-gather(bf16[128,128]{1,0:T(8,128)(2,1)} %param.15), channel_id=1, replica_groups=mesh['ctx'=16,'head'=2] {'ctx'}, dimensions={0}, use_global_device_ids=true | all-gather | bytes 557056 | tf_op jit(solution)/shard_map/all_gather | solution.py:139
  58.1 1.3 conditional.3
  58.1 0.7 broadcast_in_dim.48
  58.8 0.6 broadcast_in_dim.57
  59.4 1.0 fusion.86
  60.4 0.9 fusion.92
  61.3 1.0 fusion.88
  62.2 0.3 fusion.102
  62.5 1.0 convolution_bitcast_fusion.2
  63.5 10.6 %conditional.4 = (f32[128,4]{0,1:T(4,128)}, f32[128,4,128]{0,2,1:T(8,128)S(1)}) conditional(s32[]{:T(128)} %convert_element_type.80, () %tuple.55, (s32[]{:T(128)}, s32[128]{0:T(128)S(1)}, bf16[128,4,128]{0,2,1:T(8,128)(2,1)S(1)}, bf16[2048,128]{1,0:T(8,128)(2,1)S(1)}, bf16[2048,128]{1,0:T(8,128)(2,1)S(1)}) %tuple.110), branch_computations={%region_16.17_spmd, %region_17.25_spmd} | conditional | flops 548667136 | bytes 36583032 | solution.py:118
  63.5 2.7 %convolution_multiply_fusion = f32[128,4,2048]{2,0,1:T(8,128)} fusion(bf16[128,4,128]{0,2,1:T(8,128)(2,1)S(1)} %get-tuple-element.249, bf16[2048,128]{1,0:T(8,128)(2,1)S(1)} %get-tuple-element.188), kind=kOutput, calls=%fused_computation.38 | convolution fusion | flops 269484032 | bytes 4849664 | tf_op jit(solution)/shard_map/cond/branch_1_fun/rgd,kd->rgk/dot_general | solution.py:81
  66.2 0.7 fusion.95
  67.5 6.4 %conditional = (f32[128,4]{0,1:T(4,128)}, f32[128,4,128]{2,0,1:T(8,128)S(1)}) conditional(s32[]{:T(128)} %convert_element_type.60, (f32[128,4,2048]{2,0,1:T(8,128)}, bf16[2048,128]{1,0:T(8,128)(2,1)S(1)}) %tuple.43, (s32[128]{0:T(128)S(1)}, f32[128,4,2048]{2,0,1:T(8,128)}, bf16[2048,128]{1,0:T(8,128)(2,1)S(1)}) %tuple.44), branch_computations={%region_19.21_spmd, %region_22.24_spmd} | conditional | flops 279182848 | bytes 31207980 | solution.py:85
  67.5 0.2 iota_compare_fusion.1
  67.8 2.9 %select_reduce_fusion = f32[128,4]{0,1:T(4,128)S(1)} fusion(f32[128,4,2048]{2,0,1:T(8,128)} %get-tuple-element.183, pred[128,2048]{1,0:T(8,128)(4,1)S(1)} %iota_compare_fusion.1), kind=kLoop, calls=%fused_computation.28 | loop fusion | flops 2096640 | bytes 4458496 | tf_op jit(solution)/shard_map/cond/branch_1_fun/cond/branch_1_fun/reduce_max | solution.py:53
  70.6 0.3 copy-done.2
  71.0 1.2 fusion.22
  72.2 1.7 fusion.21
  73.9 0.1 copy.82
  74.1 2.1 multiply_reduce_fusion
  76.2 0.9 convolution_convert_fusion
  77.1 0.0 all-reduce.3.cloned.1.call-start
  77.2 0.3 fusion.90
  77.5 30.0 %all-gather.2 = bf16[16,4,128]{2,1,0:T(4,128)(2,1)S(1)} all-gather(bf16[1,4,128]{2,1,0:T(4,128)(2,1)S(1)} %convert_bitcast_fusion), channel_id=3, replica_groups=mesh['ctx'=16,'head'=2] {'ctx'}, dimensions={0}, use_global_device_ids=true | all-gather | bytes 17408 | tf_op jit(solution)/shard_map/all_gather | solution.py:12
  107.5 0.2 fusion.45
  107.7 0.2 fusion.76
  107.9 1.4 fusion.40
  109.3 0.1 fusion.63
  109.5 1.8 convolution_bitcast_fusion.3
  111.3 0.2 fusion.91
  111.5 16.7 %all-gather.5.cloned.1.call-done = bf16[64,128,128]{2,1,0:T(8,128)(2,1)} async-done(((bf16[4,128,128]{2,1,0:T(8,128)(2,1)}), bf16[64,128,128]{2,1,0:T(8,128)(2,1)}) %all-gather.5.cloned.1.call-update) | async-done | bytes 2097168 | tf_op jit(solution)/shard_map/all_gather | solution.py:12
  128.2 17.4 %while.18 = (s32[]{:T(128)}, f32[4,128,128]{2,1,0:T(8,128)S(1)}, f32[4,128]{1,0:T(4,128)S(1)}, s32[]{:T(128)}, bf16[16,4,128,128]{3,2,1,0:T(8,128)(2,1)}, /*inde...) while((s32[]{:T(128)}, f32[4,128,128]{2,1,0:T(8,128)S(1)}, ...), condition=%wide.region_30.31_spmd.clone, body=%wide.region_29.30_spmd.clone.sunk | while | flops 264200 | bytes 660657 | solution.py:30
  128.2 1.0 add_select_fusion.4
  129.3 1.0 add_select_fusion.4
  130.4 1.0 add_select_fusion.4
  131.5 1.0 add_select_fusion.4
  132.6 1.0 add_select_fusion.4
  133.6 1.0 add_select_fusion.4
  134.7 1.0 add_select_fusion.4
  135.8 1.0 add_select_fusion.4
  136.9 1.0 add_select_fusion.4
  138.0 1.0 add_select_fusion.4
  139.1 1.0 add_select_fusion.4
  140.2 1.0 add_select_fusion.4
  141.3 1.0 add_select_fusion.4
  142.4 1.0 add_select_fusion.4
  143.5 1.0 add_select_fusion.4
  144.5 1.0 add_select_fusion.4
  145.6 0.3 fusion.38
  145.9 0.1 fusion.60
  146.1 0.8 convolution_bitcast_fusion.5
  146.9 38.6 %psum.23 = f32[]{:T(128)} all-reduce(f32[]{:T(128)} %get-tuple-element.259), channel_id=1, replica_groups=mesh['ctx'=16,'head'=2] {'ctx','head'}, use_global_device_ids=true, to_apply=%region_35.36 | all-reduce | flops 1 | bytes 8 | tf_op jit(solution)/shard_map/psum | solution.py:209
  185.5 0.8 copy.60
  187.0 47.8 %all-reduce.3.cloned.1.call-done = (f32[4,128,64]{1,2,0:T(8,128)}, f32[4,128,64]{1,2,0:T(8,128)}) async-done(((f32[4,128,64]{1,2,0:T(8,128)}, f32[4,128,64]{1,2,0:T(8,128)}), (f32[4,128,64]{1,2,0:T(8,128)}, f32[4,128,64]{1,2,0:T(8,128)})) %all-reduce.3.cloned.1.call-update) | async-done | bytes 262160 | tf_op jit(solution)/shard_map/psum | solution.py:208
  234.7 1.6 copy.106
  236.3 1.6 copy.107
  (46 shorter events, 0.4 us)
Async XLA Ops:
  7.2 1.1 copy-start
  7.2 121.0 %all-gather.5.cloned.1.call-start = ((), (), s32[]{:S(2)}) async-start(), calls=%async_computation | async-start | bytes 2228224 | tf_op jit(solution)/shard_map/all_gather | solution.py:12
  63.5 44.0 %copy-start.6 = (bf16[128,128]{1,0:T(8,128)(2,1)S(1)}, bf16[128,128]{1,0:T(8,128)(2,1)}, u32[]{:S(2)}) copy-start(bf16[128,128]{1,0:T(8,128)(2,1)} %param.15) | copy-start | bytes 98308
  67.5 3.5 %copy-start.2 = (f32[128,4,2048]{2,0,1:T(8,128)S(1)}, f32[128,4,2048]{2,0,1:T(8,128)}, u32[]{:S(2)}) copy-start(f32[128,4,2048]{2,0,1:T(8,128)} %get-tuple-element.183) | copy-start | bytes 12582916 | tf_op jit(solution)/shard_map/cond/branch_1_fun/cond
  74.1 35.2 %copy-start.5 = (f32[128,4,64]{0,2,1:T(8,128)S(1)}, f32[128,4,64]{0,2,1:T(8,128)}, u32[]{:S(2)}) copy-start(f32[128,4,64]{0,2,1:T(8,128)} %get-tuple-element.292) | copy-start | bytes 393220
  74.1 35.2 %copy-start.11 = (f32[128,4]{0,1:T(4,128)S(1)}, f32[128,4]{0,1:T(4,128)}, u32[]{:S(2)}) copy-start(f32[128,4]{0,1:T(4,128)} %get-tuple-element.291) | copy-start | bytes 6148
  74.1 35.4 %copy-start.10 = (f32[128,4]{0,1:T(4,128)S(1)}, f32[128,4]{0,1:T(4,128)}, u32[]{:S(2)}) copy-start(f32[128,4]{0,1:T(4,128)} %get-tuple-element.289) | copy-start | bytes 6148
  77.1 157.6 %all-reduce.3.cloned.1.call-start = ((), (), s32[]{:S(2)}) async-start(), calls=%async_computation.1 | async-start | bytes 524288 | tf_op jit(solution)/shard_map/psum | solution.py:208
  107.7 38.2 %copy-start.4 = (f32[128,4,64]{0,2,1:T(8,128)S(1)}, f32[128,4,64]{0,2,1:T(8,128)}, u32[]{:S(2)}) copy-start(f32[128,4,64]{0,2,1:T(8,128)} %get-tuple-element.288) | copy-start | bytes 393220
  107.7 38.2 %copy-start.9 = (f32[128,4]{0,1:T(4,128)S(1)}, f32[128,4]{0,1:T(4,128)}, u32[]{:S(2)}) copy-start(f32[128,4]{0,1:T(4,128)} %get-tuple-element.287) | copy-start | bytes 6148
  109.3 36.8 %copy-start.7 = (bf16[128,128]{1,0:T(8,128)(2,1)S(1)}, bf16[128,128]{1,0:T(8,128)(2,1)}, u32[]{:S(2)}) copy-start(bf16[128,128]{1,0:T(8,128)(2,1)} %param.14) | copy-start | bytes 98308
  109.3 36.8 %copy-start.8 = (f32[128,4]{0,1:T(4,128)S(1)}, f32[128,4]{0,1:T(4,128)}, u32[]{:S(2)}) copy-start(f32[128,4]{0,1:T(4,128)} %get-tuple-element.285) | copy-start | bytes 6148
Sparse Core Ops, SparseCore 0:
  77.2 50.9 all-gather.4
  147.1 87.6 all-reduce.2
where the time goes:
time: 247 us; the launch traced here: 246 us
  blocking collectives  113 us (46%)
  waiting for transfers between devices  64.5 us (26%)
  other arithmetic  26.8 us (11%)
  matrix products  18 us (7%)
  between operations  16.1 us (7%)
  local copies, waits for them, and re-layouts  6.73 us (3%)
    psum x1, waiting for transfers between devices, on_device(): grad_query, grad_key = lax.psum((weight_q, weight_k), 'ctx')  47.8 us
    psum x1, blocking collectives, on_device(): error_all = lax.psum(error_local, ('ctx', 'head'))  38.6 us
    all_gather x1, blocking collectives, entering(): lax.all_gather(part.astype(kind), axis)  30 us
    all_gather x1, blocking collectives, on_device(): lax.all_gather(keys, 'ctx', axis=0, tiled=True)  24.8 us
    all_gather x1, blocking collectives, on_device(): lax.all_gather(values, 'ctx', axis=0, tiled=True)  19.1 us
    select_n x32, other arithmetic, turn(): return jax.tree.map(lambda a, b: jnp.where(reached, a, b), new, before)  16.9 us
    all_gather x1, waiting for transfers between devices, entering(): lax.all_gather(part.astype(kind), axis)  16.7 us
    unnamed x22, local copies, waits for them, and re-layouts  4.98 us
  transfers between devices with their start and end apart: 2, of which 2 were waited for; matrix products, arithmetic and copies ran while one was open for 2% of the time, Pallas kernels for 0%

commit v1 on v0

v1 whole, which is shorter than its diff:
```python
import functools
import math

import jax
import jax.numpy as jnp
from jax import lax
from jax.experimental import pallas as pl
from jax.experimental.pallas import tpu as pltpu
from jax.sharding import PartitionSpec as P

MESH = pl.DeviceIdType.MESH
F32 = jnp.float32
BF16 = jnp.bfloat16
PLANE = 4


def dot(a, b):
    return lax.dot_general(a, b, (((1,), (0,)), ((), ())), preferred_element_type=F32)


def dot_nt(a, b):
    return lax.dot_general(a, b, (((1,), (1,)), ((), ())), preferred_element_type=F32)


def feature_map(logits):
    high = jnp.max(logits, axis=0, keepdims=True)
    low = jnp.min(logits, axis=0, keepdims=True)
    pos = jnp.exp(logits - high)
    neg = jnp.exp(low - logits)
    pos = pos * (1.0 / jnp.sum(pos, axis=0, keepdims=True))
    neg = neg * (1.0 / jnp.sum(neg, axis=0, keepdims=True))
    return jnp.concatenate([pos, neg], axis=0)


def feature_grad(both, upstream):
    width = both.shape[0] // 2
    pos, neg = both[:width], both[width:]
    up_pos, up_neg = upstream[:width], upstream[width:]
    return pos * (up_pos - jnp.sum(up_pos * pos, axis=0, keepdims=True)) - neg * (
        up_neg - jnp.sum(up_neg * neg, axis=0, keepdims=True)
    )


def split(array):
    high = array.astype(BF16)
    return high, (array - high.astype(F32)).astype(BF16)


def kernel(
    dims,
    q_ref, k_ref, v_ref, fq_ref, fk_ref,
    student_ref, gq_ref, gk_ref, err_ref,
    kv, wk, qs, top, total, acc, s_t, s_n, fqp, fkp, dfq, ldfk,
    st_out, st_in, st_fin, st_res, gq_out, gq_in, gk_out, gk_in, g_fin, g_res, e_out, e_in,
    z_send, x_send, c_send, kv_recv, a_send, a_recv, b_send, b_recv,
    q_send, q_recv, k_send, k_recv, g_send, g_recv, e_send, e_recv,
):
    n, heads_axis, rows, heads, hd, feat, state_pieces, grad_pieces = dims
    me = lax.axis_index("ctx")
    my_head = lax.axis_index("head")
    feat2 = 2 * feat
    place = me % PLANE
    level = me // PLANE
    levels = n // PLANE
    core_mate = me + 1 - 2 * (me % 2)
    x_mate = me + 2 - 4 * ((me // 2) % 2)
    span = PLANE * rows

    def copy(src, dst, send, recv, target):
        return pltpu.make_async_remote_copy(
            src_ref=src, dst_ref=dst, send_sem=send, recv_sem=recv,
            device_id=(target, my_head), device_id_type=MESH,
        )

    def peers(body):
        def step(k, carry):
            body((me + k) % n)
            return carry

        lax.fori_loop(1, n, step, 0)

    def guarded(index, pieces, body):
        if pieces == n:
            body()
        else:
            pl.when(index < pieces)(body)

    def head_mates(body):
        def step(k, carry):
            body((my_head + k) % heads_axis)
            return carry

        lax.fori_loop(1, heads_axis, step, 0)

    barrier = pltpu.get_barrier_semaphore()
    peers(lambda p: pl.semaphore_signal(barrier, inc=1, device_id=(p, my_head), device_id_type=MESH))
    head_mates(lambda p: pl.semaphore_signal(barrier, inc=1, device_id=(me, p), device_id_type=MESH))
    kv[me, 0] = k_ref[...]
    v_t = v_ref[...].astype(F32).T.astype(BF16)
    kv[me, 1] = v_t
    pl.semaphore_wait(barrier, n - 1 + heads_axis - 1)

    def z_copy(up):
        return copy(kv.at[me], kv.at[me], z_send.at[up], kv_recv.at[me], up * PLANE + place)

    def kv_copy(block, send, target):
        return copy(kv.at[block], kv.at[block], send, kv_recv.at[block], target)

    def x_copy(h):
        return kv_copy(h * PLANE + place, x_send.at[h], x_mate)

    def c_copy(h):
        return kv_copy(h * PLANE + place, c_send.at[0, h], core_mate)

    def f_copy(h):
        return kv_copy(h * PLANE + x_mate % PLANE, c_send.at[1, h], core_mate)

    def kv_wait(block):
        kv_copy(block, z_send.at[0], core_mate).wait_recv()

    def loop(low, high, body):
        def step(i, carry):
            body(i)
            return carry

        lax.fori_loop(low, high, step, 0)

    x_copy(level).start()
    c_copy(level).start()
    loop(level + 1, levels, lambda up: z_copy(up).start())

    def weight_rows(ref):
        return jnp.concatenate(
            [ref[g].astype(F32).T.astype(BF16) for g in range(heads)], axis=0
        )

    w_k = weight_rows(fk_ref)
    wk[...] = w_k
    w_q = weight_rows(fq_ref)
    own_k = dot_nt(w_k, k_ref[...])
    for g in range(heads):
        q_g = q_ref[:, g * hd : (g + 1) * hd]
        qs[g * rows : (g + 1) * rows, :] = q_g
        fqp[g] = feature_map(dot_nt(w_q[g * feat : (g + 1) * feat], q_g))
        fkp[g] = feature_map(own_k[g * feat : (g + 1) * feat])
    top[...] = jnp.full_like(top, -1e30)
    total[...] = jnp.zeros_like(total)
    acc[...] = jnp.zeros_like(acc)
    s_t[...] = jnp.zeros_like(s_t)
    s_n[...] = jnp.zeros_like(s_n)

    def relay(t):
        h = level - 1 - t
        kv_wait(h * PLANE + place)
        x_copy(h).start()
        c_copy(h).start()

    loop(0, level, relay)

    def pass_on(t):
        h = level - t
        kv_wait(h * PLANE + x_mate % PLANE)
        f_copy(h).start()

    loop(0, level + 1, pass_on)

    scale = hd ** (-0.5) / math.log(2.0)
    ones = jnp.ones((hd, span), BF16)

    def absorb(t):
        h = level - t
        kv_wait(h * PLANE + core_mate % PLANE)
        kv_wait(h * PLANE + core_mate % PLANE + 2 - 4 * ((core_mate // 2) % 2))
        keys = kv[pl.ds(h * PLANE, PLANE), 0].reshape(span, hd)
        vals = jnp.concatenate([kv[h * PLANE + b, 1] for b in range(PLANE)], axis=1)
        key_pos = h * span + lax.broadcasted_iota(jnp.int32, (span, rows), 0)
        query_pos = me * rows + lax.broadcasted_iota(jnp.int32, (span, rows), 1)
        allowed = key_pos <= query_pos
        for g in range(heads):
            scores = dot_nt(keys, qs[g * rows : (g + 1) * rows, :])
            scores = jnp.where(allowed, scores, -1e30)
            old = top[g]
            new = jnp.maximum(old, jnp.max(scores, axis=0, keepdims=True))
            top[g] = new
            shrink = jnp.exp2((old - new) * scale)
            weights = jnp.exp2((scores - new) * scale)
            total[g] = total[g] * shrink + jnp.sum(weights, axis=0, keepdims=True)
            acc[g] = acc[g] * shrink + dot(vals, weights.astype(BF16))
        logits = dot_nt(wk[...], keys)
        before = h * span + lax.broadcasted_iota(jnp.int32, (feat2, span), 1) < me * rows
        maps = jnp.concatenate(
            [
                jnp.where(before, feature_map(logits[g * feat : (g + 1) * feat]), 0.0).astype(BF16)
                for g in range(heads)
            ],
            axis=0,
        )
        wide = jnp.concatenate([vals, ones], axis=0)
        s_t[...] += dot_nt(wide, maps)
        s_n[...] += dot_nt(maps, wide)

    loop(0, level + 1, absorb)

    key_row = lax.broadcasted_iota(jnp.int32, (rows, rows), 0)
    query_col = lax.broadcasted_iota(jnp.int32, (rows, rows), 1)
    causal = key_row <= query_col
    per_head = state_pieces // heads
    piece = heads * feat2 // state_pieces
    squares = jnp.zeros((hd, rows), F32)
    norm_rows = []
    values = v_ref[...]
    for g in range(heads):
        fq_t = fqp[g].astype(BF16)
        fk_t = fkp[g].astype(BF16)
        fk_n = fkp[g].T.astype(BF16)
        amat = jnp.where(causal, dot(fk_n, fq_t), 0.0)
        high, low = split(s_t[:, g * feat2 : (g + 1) * feat2])
        prior = dot(jnp.concatenate([high, low], axis=1), jnp.concatenate([fq_t, fq_t], axis=0))
        numer = dot(v_t, amat.astype(BF16)) + prior[:hd]
        denom = jnp.sum(amat, axis=0, keepdims=True) + prior[hd : hd + 1]
        inverse = 1.0 / denom
        y = numer * inverse
        student_ref[:, g * hd : (g + 1) * hd] = y.T.astype(BF16)
        diff = y - acc[g] * (1.0 / total[g])
        squares = squares + diff * diff
        dy = 2.0 * diff
        dnumer = dy * inverse
        dden = -jnp.sum(dy * y, axis=0, keepdims=True) * inverse
        dnb = dnumer.astype(BF16)
        dmat = jnp.where(causal, dot(values, dnb) + dden, 0.0).astype(BF16)
        state = dot_nt(fq_t, dnb).astype(BF16)
        st_out[g * per_head : (g + 1) * per_head, :piece, :] = state.reshape(per_head, piece, hd)
        d_high, d_low = split(jnp.broadcast_to(dden, (16, rows)))
        norm_rows.append(dot_nt(d_high, fq_t) + dot_nt(d_low, fq_t))
        high, low = split(s_n[g * feat2 : (g + 1) * feat2, :hd])
        dfq[g] = (
            dot(jnp.concatenate([fk_t, high, low], axis=1), jnp.concatenate([dmat, dnb, dnb], axis=0))
            + s_n[g * feat2 : (g + 1) * feat2, hd:] * dden
        )
        ldfk[g] = dot_nt(fq_t, dmat)
    error = jnp.sum(jnp.sum(squares, axis=0, keepdims=True), axis=1, keepdims=True)
    extra_row = lax.broadcasted_iota(jnp.int32, (16, hd), 0)

    def with_error(norms, value):
        first = value.astype(BF16).astype(F32)
        return jnp.where(
            extra_row < 8, norms, jnp.where(extra_row < 12, first, value - first)
        ).astype(BF16)

    error = jnp.broadcast_to(error, (16, hd))
    for g in range(heads):
        extra = with_error(norm_rows[g], error)
        for p in range(g * per_head, (g + 1) * per_head):
            st_out[p, piece:, :] = extra

    def a_copy(p, s):
        return copy(st_out.at[p], st_in.at[s], a_send.at[p], a_recv.at[s], p)

    peers(lambda p: guarded(p, state_pieces, lambda: a_copy(p, me).start()))

    grad_rows = heads * feat // grad_pieces
    grad_per_head = grad_pieces // heads
    for g in range(heads):
        dlq = feature_grad(fqp[g], dfq[g]).astype(BF16)
        part = dot(dlq, qs[g * rows : (g + 1) * rows, :]).astype(BF16)
        gq_out[g * grad_per_head : (g + 1) * grad_per_head] = part.reshape(
            grad_per_head, grad_rows, hd
        )

    def q_copy(p, s):
        return copy(gq_out.at[p], gq_in.at[s], q_send.at[p], q_recv.at[s], p)

    def b_copy(d, s):
        return copy(st_fin.at[d], st_res.at[s], b_send.at[d], b_recv.at[s], d)

    def reduce_states():
        st_in[me] = st_out[me]
        peers(lambda s: a_copy(0, s).wait_recv())
        extras = jnp.sum(st_in[:, piece:, :].astype(F32), axis=0)
        summed = jnp.sum(jnp.where(extra_row < 8, 0.0, extras), axis=0, keepdims=True) * 0.25
        summed = jnp.broadcast_to(summed, (16, hd))

        def suffix(t, carry):
            states, norms = carry
            d = n - 1 - t
            st_fin[d, :piece, :] = states.astype(BF16)
            st_fin[d, piece:, :] = with_error(norms, summed)
            return (
                states + st_in[d, :piece, :].astype(F32),
                norms + st_in[d, piece:, :].astype(F32),
            )

        lax.fori_loop(
            0, n, suffix, (jnp.zeros((piece, hd), F32), jnp.zeros((16, hd), F32))
        )
        peers(lambda d: b_copy(d, me).start())
        st_res[me] = st_fin[me]

    guarded(me, state_pieces, reduce_states)
    peers(lambda p: guarded(p, grad_pieces, lambda: q_copy(p, me).start()))
    peers(lambda s: guarded(s, state_pieces, lambda: b_copy(0, s).wait_recv()))

    last = st_res[0, piece:, :].astype(F32)
    e_out[...] = jnp.broadcast_to(
        jnp.sum(jnp.where(extra_row < 8, 0.0, last), axis=0, keepdims=True) * 0.25, e_out.shape
    )

    def e_copy(p, s):
        return pltpu.make_async_remote_copy(
            src_ref=e_out, dst_ref=e_in.at[s], send_sem=e_send.at[p], recv_sem=e_recv.at[s],
            device_id=(me, p), device_id_type=MESH,
        )

    for g in range(heads):
        later = st_res[g * per_head : (g + 1) * per_head, :piece, :].reshape(feat2, hd)
        norm = jnp.broadcast_to(
            st_res[g * per_head, piece : piece + 16, :].astype(F32)[:1], (rows, feat2)
        ).T
        dfk = ldfk[g] + dot(later, v_t) + norm
        dlk = feature_grad(fkp[g], dfk).astype(BF16)
        part = dot(dlk, k_ref[...]).astype(BF16)
        gk_out[g * grad_per_head : (g + 1) * grad_per_head] = part.reshape(
            grad_per_head, grad_rows, hd
        )

    def k_copy(p, s):
        return copy(gk_out.at[p], gk_in.at[s], k_send.at[p], k_recv.at[s], p)

    def g_copy(d, s):
        return copy(g_fin, g_res.at[s], g_send.at[d], g_recv.at[s], d)

    peers(lambda p: guarded(p, grad_pieces, lambda: k_copy(p, me).start()))
    head_mates(lambda p: e_copy(p, my_head).start())

    def reduce_grads():
        gq_in[me] = gq_out[me]
        gk_in[me] = gk_out[me]
        peers(lambda s: q_copy(0, s).wait_recv())
        g_fin[:grad_rows] = jnp.sum(gq_in[...].astype(F32), axis=0).astype(BF16)
        peers(lambda s: k_copy(0, s).wait_recv())
        g_fin[grad_rows:] = jnp.sum(gk_in[...].astype(F32), axis=0).astype(BF16)
        peers(lambda d: g_copy(d, me).start())
        g_res[me] = g_fin[...]

    guarded(me, grad_pieces, reduce_grads)

    e_in[my_head] = e_out[...]
    head_mates(lambda s: e_copy(0, s).wait_recv())
    entries = n * rows * heads * heads_axis * hd
    err_ref[...] = jnp.sum(e_in[...], axis=0) / entries
    head_mates(lambda p: e_copy(p, my_head).wait_send())
    x_copy(level).wait_send()
    c_copy(level).wait_send()
    loop(level + 1, levels, lambda up: z_copy(up).wait_send())

    def relay_end(t):
        x_copy(t).wait_send()
        c_copy(t).wait_send()

    loop(0, level, relay_end)
    loop(0, level + 1, lambda t: f_copy(t).wait_send())
    peers(lambda p: guarded(p, state_pieces, lambda: a_copy(p, me).wait_send()))
    guarded(me, state_pieces, lambda: peers(lambda d: b_copy(d, me).wait_send()))
    peers(lambda p: guarded(p, grad_pieces, lambda: q_copy(p, me).wait_send()))
    peers(lambda p: guarded(p, grad_pieces, lambda: k_copy(p, me).wait_send()))
    peers(lambda s: guarded(s, grad_pieces, lambda: g_copy(0, s).wait_recv()))
    for g in range(heads):
        both = g_res[g * grad_per_head : (g + 1) * grad_per_head].astype(F32)
        gq_ref[g] = both[:, :grad_rows].reshape(feat, hd).T
        gk_ref[g] = both[:, grad_rows:].reshape(feat, hd).T
    guarded(me, grad_pieces, lambda: peers(lambda d: g_copy(d, me).wait_send()))


def on_device(queries, keys, values, feat_q, feat_k):
    rows, hd = keys.shape
    heads, _, feat = feat_q.shape
    n = lax.axis_size("ctx")
    heads_axis = lax.axis_size("head")
    feat2 = 2 * feat
    state_pieces = min(n, heads * feat2 // 16)
    grad_pieces = min(n, heads * feat // 16)
    dims = (n, heads_axis, rows, heads, hd, feat, state_pieces, grad_pieces)
    piece = heads * feat2 // state_pieces + 16
    grad_rows = heads * feat // grad_pieces
    levels = n // PLANE
    dma = pltpu.SemaphoreType.DMA
    vmem = pl.BlockSpec(memory_space=pltpu.VMEM)
    student, grad_q, grad_k, error = pl.pallas_call(
        functools.partial(kernel, dims),
        out_shape=(
            jax.ShapeDtypeStruct((rows, heads * hd), BF16),
            jax.ShapeDtypeStruct((heads, hd, feat), F32),
            jax.ShapeDtypeStruct((heads, hd, feat), F32),
            jax.ShapeDtypeStruct((8, hd), F32),
        ),
        in_specs=[vmem] * 5,
        out_specs=(vmem,) * 4,
        scratch_shapes=[
            pltpu.VMEM((n, 2, rows, hd), BF16),
            pltpu.VMEM((heads * feat, hd), BF16),
            pltpu.VMEM((heads * rows, hd), BF16),
            pltpu.VMEM((heads, 1, rows), F32),
            pltpu.VMEM((heads, 1, rows), F32),
            pltpu.VMEM((heads, hd, rows), F32),
            pltpu.VMEM((2 * hd, heads * feat2), F32),
            pltpu.VMEM((heads * feat2, 2 * hd), F32),
            pltpu.VMEM((heads, feat2, rows), F32),
            pltpu.VMEM((heads, feat2, rows), F32),
            pltpu.VMEM((heads, feat2, rows), F32),
            pltpu.VMEM((heads, feat2, rows), F32),
            pltpu.VMEM((state_pieces, piece, hd), BF16),
            pltpu.VMEM((n, piece, hd), BF16),
            pltpu.VMEM((n, piece, hd), BF16),
            pltpu.VMEM((state_pieces, piece, hd), BF16),
            pltpu.VMEM((grad_pieces, grad_rows, hd), BF16),
            pltpu.VMEM((n, grad_rows, hd), BF16),
            pltpu.VMEM((grad_pieces, grad_rows, hd), BF16),
            pltpu.VMEM((n, grad_rows, hd), BF16),
            pltpu.VMEM((2 * grad_rows, hd), BF16),
            pltpu.VMEM((grad_pieces, 2 * grad_rows, hd), BF16),
            pltpu.VMEM((8, hd), F32),
            pltpu.VMEM((heads_axis, 8, hd), F32),
            dma((levels,)),
            dma((levels,)),
            dma((2, levels)),
            dma((n,)),
            dma((n,)),
            dma((n,)),
            dma((n,)),
            dma((n,)),
            dma((n,)),
            dma((n,)),
            dma((n,)),
            dma((n,)),
            dma((n,)),
            dma((n,)),
            dma((heads_axis,)),
            dma((heads_axis,)),
        ],
        compiler_params=pltpu.CompilerParams(
            collective_id=0, has_side_effects=True, vmem_limit_bytes=40 * 1024 * 1024
        ),
    )(queries, keys, values, feat_q, feat_k)
    return student, grad_q, grad_k, error[0, 0]


def solution(mesh):
    in_specs = (
        P("ctx", "head"),
        P("ctx", "head"),
        P("ctx", "head"),
        P("head", None, None),
        P("head", None, None),
    )
    out_specs = (P("ctx", "head"), P("head", None, None), P("head", None, None), P())
    return jax.shard_map(
        on_device, mesh=mesh, in_specs=in_specs, out_specs=out_specs, check_vma=False
    )
```

time: 247 us -> 53.2 us (0.22)
  blocking collectives: 113 us -> 0 us
  waiting for transfers between devices: 64.5 us -> 0 us
  Pallas kernels: 0 us -> 47.8 us
  other arithmetic: 26.8 us -> 0 us
  matrix products: 18 us -> 0 us
  between operations: 16.1 us -> 0.69 us
    all_gather x3 -> x0, blocking collectives: 73.9 us -> none  [the longest x1 30 us: entering(): lax.all_gather(part.astype(kind), axis)]
    psum x1 -> x0, waiting for transfers between devices: 47.8 us -> none  [on_device(): grad_query, grad_key = lax.psum((weight_q, weight_k), 'ctx')]
    pallas_call x0 -> x1, Pallas kernels: none -> 47.8 us  [on_device(): pl.pallas_call(functools.partial(kernel, dims), out_shape=(jax.ShapeDtype...]
    psum x1 -> x0, blocking collectives: 38.6 us -> none  [on_device(): error_all = lax.psum(error_local, ('ctx', 'head'))]
    select_n x32 -> x0, other arithmetic: 16.9 us -> none  [turn(): return jax.tree.map(lambda a, b: jnp.where(reached, a, b), new, before)]
    all_gather x1 -> x0, waiting for transfers between devices: 16.7 us -> none  [entering(): lax.all_gather(part.astype(kind), axis)]
    dot_general x15 -> x0, matrix products: 14.1 us -> none  [the longest x1 2.66 us: attend(): jnp.einsum('rgd,kd->rgk', query_rows, key_piece, preferred_element_type=j...]
    reduce_max x1 -> x0, other arithmetic: 2.87 us -> none  [masked_update(): new_max = jnp.maximum(running, jnp.max(score_matrix, axis=-1))]
  transfers between devices with their start and end apart: 2 -> 0, of which waited for: 2 -> 0; matrix products, arithmetic and copies ran while one was open for 2% -> 0% of each run, Pallas kernels for 0% -> 0%
where the time goes in v1:
time: 53.2 us; the launch traced here: 53.1 us
  Pallas kernels  47.8 us (90%)
  local copies, waits for them, and re-layouts  4.59 us (9%)
  between operations  0.69 us (1%)
    pallas_call x1, Pallas kernels, on_device(): pl.pallas_call(functools.partial(kernel, dims), out_shape=(jax.ShapeDtype...  47.8 us
    unnamed x13, local copies, waits for them, and re-layouts  4.08 us

profile of v1, /device:TPU:0, one launch (start us, length us, event | category | flops | bytes accessed | tf_op | source)
XLA Modules:
  0.0 53.1 jit_solution(12761984605932490590)
XLA Ops:
  0.6 0.0 copy-start.3
  0.6 1.0 %copy.9.fq_ref = bf16[4,128,64]{2,1,0:T(8,128)(2,1)S(1)} copy(bf16[4,128,64]{1,2,0:T(8,128)(2,1)} %param.8) | data formatting | bytes 131072 | tf_op args[3]
  1.6 0.0 copy-done.3
  1.6 0.0 copy-start
  1.7 0.0 copy-start.1
  1.7 0.0 copy-start.2
  1.7 0.1 copy.10.fk_ref
  1.8 0.7 %copy-done = bf16[128,512]{1,0:T(8,128)(2,1)S(1)} copy-done((bf16[128,512]{1,0:T(8,128)(2,1)S(1)}, bf16[128,512]{1,0:T(8,128)(2,1)}, u32[]{:S(2)}) %copy-start) | copy-done | bytes 131096
  2.6 0.0 copy-done.1
  2.6 0.0 copy-done.2
  2.6 47.8 %shard_map.84 = (bf16[128,512]{1,0:T(8,128)(2,1)S(1)}, f32[4,128,64]{2,1,0:T(8,128)S(1)}, f32[4,128,64]{2,1,0:T(8,128)S(1)}, f32[8,128]{1,0:T(8,128)S(1)}) custom-call(bf16[128,512]{1,0:T(8,128)(2,1)S(1)} %copy-done, bf16[128,128]{1,0:T(8,128)(2,1)S(1)} %copy-done.1, bf16[128,128]{1,0:T(8,128)(2,1)S(1)} %copy-done.2, bf16[4,128,64]{2,1,0:T(8,128)(2,1)S(1)} %copy.9.fq_ref, ...), custom_call_target="tpu_custom_call" | custom-call | tf_op jit(solution)/shard_map/pallas_call | solution.py:388
  50.3 0.5 slice.3
  50.9 0.8 %copy.11 = f32[4,128,64]{1,2,0:T(8,128)} copy(f32[4,128,64]{2,1,0:T(8,128)S(1)} %get-tuple-element.13) | data formatting | bytes 262144
  51.6 0.8 %copy.12 = f32[4,128,64]{1,2,0:T(8,128)} copy(f32[4,128,64]{2,1,0:T(8,128)S(1)} %get-tuple-element.14) | data formatting | bytes 262144
  52.4 0.7 %copy.14 = bf16[128,512]{1,0:T(8,128)(2,1)} copy(bf16[128,512]{1,0:T(8,128)(2,1)S(1)} %get-tuple-element.20) | data formatting | bytes 262144
Async XLA Ops:
  0.6 1.0 %copy-start.3 = (bf16[4,128,64]{1,2,0:T(8,128)(2,1)S(1)}, bf16[4,128,64]{1,2,0:T(8,128)(2,1)}, u32[]{:S(2)}) copy-start(bf16[4,128,64]{1,2,0:T(8,128)(2,1)} %param.9) | copy-start | bytes 196612
  1.6 0.9 %copy-start = (bf16[128,512]{1,0:T(8,128)(2,1)S(1)}, bf16[128,512]{1,0:T(8,128)(2,1)}, u32[]{:S(2)}) copy-start(bf16[128,512]{1,0:T(8,128)(2,1)} %q_ref.1) | copy-start | bytes 393220
  1.7 0.9 %copy-start.1 = (bf16[128,128]{1,0:T(8,128)(2,1)S(1)}, bf16[128,128]{1,0:T(8,128)(2,1)}, u32[]{:S(2)}) copy-start(bf16[128,128]{1,0:T(8,128)(2,1)} %k_ref.1) | copy-start | bytes 98308
  1.7 0.9 %copy-start.2 = (bf16[128,128]{1,0:T(8,128)(2,1)S(1)}, bf16[128,128]{1,0:T(8,128)(2,1)}, u32[]{:S(2)}) copy-start(bf16[128,128]{1,0:T(8,128)(2,1)} %v_ref.1) | copy-start | bytes 98308

commit v2 on v1

--- a/solution.py
+++ b/solution.py
@@ -48,9 +48,10 @@
 
 def kernel(
     dims,
-    q_ref, k_ref, v_ref, fq_ref, fk_ref,
+    q_any, k_any, v_any, fq_any, fk_any,
     student_ref, gq_ref, gk_ref, err_ref,
-    kv, wk, qs, top, total, acc, s_t, s_n, fqp, fkp, dfq, ldfk,
+    q_ref, v_ref, fq_ref, fk_ref, in_sem, numl, denl, x_out, x_in, n_send, n_recv,
+    kv, qs, top, total, acc, s_t, s_n, fqp, fkp, dfq, ldfk,
     st_out, st_in, st_fin, st_res, gq_out, gq_in, gk_out, gk_in, g_fin, g_res, e_out, e_in,
     z_send, x_send, c_send, kv_recv, a_send, a_recv, b_send, b_recv,
     q_send, q_recv, k_send, k_recv, g_send, g_recv, e_send, e_recv,
@@ -92,10 +93,20 @@
 
         lax.fori_loop(1, heads_axis, step, 0)
 
+    loads = [
+        pltpu.make_async_copy(src, dst, in_sem.at[i])
+        for i, (src, dst) in enumerate(
+            ((k_any, kv.at[me, 0]), (v_any, v_ref), (fk_any, fk_ref), (q_any, q_ref), (fq_any, fq_ref))
+        )
+    ]
+    for load in loads:
+        load.start()
+
     barrier = pltpu.get_barrier_semaphore()
     peers(lambda p: pl.semaphore_signal(barrier, inc=1, device_id=(p, my_head), device_id_type=MESH))
     head_mates(lambda p: pl.semaphore_signal(barrier, inc=1, device_id=(me, p), device_id_type=MESH))
-    kv[me, 0] = k_ref[...]
+    loads[0].wait()
+    loads[1].wait()
     v_t = v_ref[...].astype(F32).T.astype(BF16)
     kv[me, 1] = v_t
     pl.semaphore_wait(barrier, n - 1 + heads_axis - 1)
@@ -129,40 +140,38 @@
     c_copy(level).start()
     loop(level + 1, levels, lambda up: z_copy(up).start())
 
-    def weight_rows(ref):
-        return jnp.concatenate(
-            [ref[g].astype(F32).T.astype(BF16) for g in range(heads)], axis=0
-        )
-
-    w_k = weight_rows(fk_ref)
-    wk[...] = w_k
-    w_q = weight_rows(fq_ref)
-    own_k = dot_nt(w_k, k_ref[...])
+    key_row = lax.broadcasted_iota(jnp.int32, (rows, rows), 0)
+    query_col = lax.broadcasted_iota(jnp.int32, (rows, rows), 1)
+    causal = key_row <= query_col
+    for load in loads[2:]:
+        load.wait()
+    w_k = fk_ref[...].reshape(heads * feat, hd)
+    w_q = fq_ref[...].reshape(heads * feat, hd)
+    own_k = dot_nt(w_k, kv[me, 0])
     for g in range(heads):
         q_g = q_ref[:, g * hd : (g + 1) * hd]
         qs[g * rows : (g + 1) * rows, :] = q_g
-        fqp[g] = feature_map(dot_nt(w_q[g * feat : (g + 1) * feat], q_g))
-        fkp[g] = feature_map(own_k[g * feat : (g + 1) * feat])
+        map_q = feature_map(dot_nt(w_q[g * feat : (g + 1) * feat], q_g))
+        map_k = feature_map(own_k[g * feat : (g + 1) * feat])
+        fqp[g] = map_q
+        fkp[g] = map_k
+        amat = jnp.where(causal, dot(map_k.T.astype(BF16), map_q.astype(BF16)), 0.0)
+        numl[g] = dot(v_t, amat.astype(BF16))
+        denl[g] = jnp.sum(amat, axis=0, keepdims=True)
     top[...] = jnp.full_like(top, -1e30)
     total[...] = jnp.zeros_like(total)
     acc[...] = jnp.zeros_like(acc)
     s_t[...] = jnp.zeros_like(s_t)
     s_n[...] = jnp.zeros_like(s_n)
 
-    def relay(t):
-        h = level - 1 - t
+    def relay(h):
         kv_wait(h * PLANE + place)
         x_copy(h).start()
         c_copy(h).start()
 
-    loop(0, level, relay)
-
-    def pass_on(t):
-        h = level - t
+    def pass_on(h):
         kv_wait(h * PLANE + x_mate % PLANE)
         f_copy(h).start()
-
-    loop(0, level + 1, pass_on)
 
     scale = hd ** (-0.5) / math.log(2.0)
     ones = jnp.ones((hd, span), BF16)
@@ -186,7 +195,7 @@
             weights = jnp.exp2((scores - new) * scale)
             total[g] = total[g] * shrink + jnp.sum(weights, axis=0, keepdims=True)
             acc[g] = acc[g] * shrink + dot(vals, weights.astype(BF16))
-        logits = dot_nt(wk[...], keys)
+        logits = dot_nt(fk_ref[...].reshape(heads * feat, hd), keys)
         before = h * span + lax.broadcasted_iota(jnp.int32, (feat2, span), 1) < me * rows
         maps = jnp.concatenate(
             [
@@ -199,11 +208,13 @@
         s_t[...] += dot_nt(wide, maps)
         s_n[...] += dot_nt(maps, wide)
 
-    loop(0, level + 1, absorb)
-
-    key_row = lax.broadcasted_iota(jnp.int32, (rows, rows), 0)
-    query_col = lax.broadcasted_iota(jnp.int32, (rows, rows), 1)
-    causal = key_row <= query_col
+    def pipeline(u):
+        pl.when(u <= level + 1)(lambda: pass_on(level - (u - 1)))
+        pl.when(u <= level)(lambda: relay(level - u))
+        pl.when(u >= 2)(lambda: absorb(u - 2))
+
+    loop(1, level + 3, pipeline)
+
     per_head = state_pieces // heads
     piece = heads * feat2 // state_pieces
     squares = jnp.zeros((hd, rows), F32)
@@ -212,12 +223,10 @@
     for g in range(heads):
         fq_t = fqp[g].astype(BF16)
         fk_t = fkp[g].astype(BF16)
-        fk_n = fkp[g].T.astype(BF16)
-        amat = jnp.where(causal, dot(fk_n, fq_t), 0.0)
         high, low = split(s_t[:, g * feat2 : (g + 1) * feat2])
         prior = dot(jnp.concatenate([high, low], axis=1), jnp.concatenate([fq_t, fq_t], axis=0))
-        numer = dot(v_t, amat.astype(BF16)) + prior[:hd]
-        denom = jnp.sum(amat, axis=0, keepdims=True) + prior[hd : hd + 1]
+        numer = numl[g] + prior[:hd]
+        denom = denl[g] + prior[hd : hd + 1]
         inverse = 1.0 / denom
         y = numer * inverse
         student_ref[:, g * hd : (g + 1) * hd] = y.T.astype(BF16)
@@ -229,7 +238,7 @@
         dnb = dnumer.astype(BF16)
         dmat = jnp.where(causal, dot(values, dnb) + dden, 0.0).astype(BF16)
         state = dot_nt(fq_t, dnb).astype(BF16)
-        st_out[g * per_head : (g + 1) * per_head, :piece, :] = state.reshape(per_head, piece, hd)
+        st_out[g * per_head : (g + 1) * per_head] = state.reshape(per_head, piece, hd)
         d_high, d_low = split(jnp.broadcast_to(dden, (16, rows)))
         norm_rows.append(dot_nt(d_high, fq_t) + dot_nt(d_low, fq_t))
         high, low = split(s_n[g * feat2 : (g + 1) * feat2, :hd])
@@ -239,24 +248,21 @@
         )
         ldfk[g] = dot_nt(fq_t, dmat)
     error = jnp.sum(jnp.sum(squares, axis=0, keepdims=True), axis=1, keepdims=True)
+    first = error.astype(BF16).astype(F32)
     extra_row = lax.broadcasted_iota(jnp.int32, (16, hd), 0)
-
-    def with_error(norms, value):
-        first = value.astype(BF16).astype(F32)
-        return jnp.where(
-            extra_row < 8, norms, jnp.where(extra_row < 12, first, value - first)
-        ).astype(BF16)
-
-    error = jnp.broadcast_to(error, (16, hd))
-    for g in range(heads):
-        extra = with_error(norm_rows[g], error)
-        for p in range(g * per_head, (g + 1) * per_head):
-            st_out[p, piece:, :] = extra
+    extra = jnp.where(extra_row < 12, first, error - first)
+    for g in range(heads):
+        extra = jnp.where(extra_row == g, norm_rows[g], extra)
+    x_out[...] = extra.astype(BF16)
+
+    def n_copy(p, s):
+        return copy(x_out, x_in.at[s], n_send.at[p], n_recv.at[s], p)
 
     def a_copy(p, s):
         return copy(st_out.at[p], st_in.at[s], a_send.at[p], a_recv.at[s], p)
 
     peers(lambda p: guarded(p, state_pieces, lambda: a_copy(p, me).start()))
+    peers(lambda p: n_copy(p, me).start())
 
     grad_rows = heads * feat // grad_pieces
     grad_per_head = grad_pieces // heads
@@ -276,34 +282,27 @@
     def reduce_states():
         st_in[me] = st_out[me]
         peers(lambda s: a_copy(0, s).wait_recv())
-        extras = jnp.sum(st_in[:, piece:, :].astype(F32), axis=0)
-        summed = jnp.sum(jnp.where(extra_row < 8, 0.0, extras), axis=0, keepdims=True) * 0.25
-        summed = jnp.broadcast_to(summed, (16, hd))
-
-        def suffix(t, carry):
-            states, norms = carry
+
+        def suffix(t, states):
             d = n - 1 - t
-            st_fin[d, :piece, :] = states.astype(BF16)
-            st_fin[d, piece:, :] = with_error(norms, summed)
-            return (
-                states + st_in[d, :piece, :].astype(F32),
-                norms + st_in[d, piece:, :].astype(F32),
-            )
-
-        lax.fori_loop(
-            0, n, suffix, (jnp.zeros((piece, hd), F32), jnp.zeros((16, hd), F32))
-        )
+            st_fin[d] = states.astype(BF16)
+            return states + st_in[d].astype(F32)
+
+        lax.fori_loop(0, n, suffix, jnp.zeros((piece, hd), F32))
         peers(lambda d: b_copy(d, me).start())
         st_res[me] = st_fin[me]
 
     guarded(me, state_pieces, reduce_states)
     peers(lambda p: guarded(p, grad_pieces, lambda: q_copy(p, me).start()))
-    peers(lambda s: guarded(s, state_pieces, lambda: b_copy(0, s).wait_recv()))
-
-    last = st_res[0, piece:, :].astype(F32)
-    e_out[...] = jnp.broadcast_to(
-        jnp.sum(jnp.where(extra_row < 8, 0.0, last), axis=0, keepdims=True) * 0.25, e_out.shape
+
+    x_in[me] = x_out[...]
+    peers(lambda s: n_copy(0, s).wait_recv())
+    extras = x_in[...].astype(F32)
+    later_norms = jnp.sum(
+        jnp.where(lax.broadcasted_iota(jnp.int32, extras.shape, 0) > me, extras, 0.0), axis=0
     )
+    summed = jnp.sum(jnp.where(extra_row < 8, 0.0, jnp.sum(extras, axis=0)), axis=0, keepdims=True)
+    e_out[...] = jnp.broadcast_to(summed * 0.25, e_out.shape)
 
     def e_copy(p, s):
         return pltpu.make_async_remote_copy(
@@ -311,14 +310,17 @@
             device_id=(me, p), device_id_type=MESH,
         )
 
-    for g in range(heads):
-        later = st_res[g * per_head : (g + 1) * per_head, :piece, :].reshape(feat2, hd)
-        norm = jnp.broadcast_to(
-            st_res[g * per_head, piece : piece + 16, :].astype(F32)[:1], (rows, feat2)
-        ).T
-        dfk = ldfk[g] + dot(later, v_t) + norm
+    head_mates(lambda p: e_copy(p, my_head).start())
+    for g in range(heads):
+        norm = jnp.broadcast_to(later_norms[g : g + 1], (rows, feat2)).T
+        ldfk[g] += norm
+
+    peers(lambda s: guarded(s, state_pieces, lambda: b_copy(0, s).wait_recv()))
+    for g in range(heads):
+        later = st_res[g * per_head : (g + 1) * per_head].reshape(feat2, hd)
+        dfk = ldfk[g] + dot(later, v_t)
         dlk = feature_grad(fkp[g], dfk).astype(BF16)
-        part = dot(dlk, k_ref[...]).astype(BF16)
+        part = dot(dlk, kv[me, 0]).astype(BF16)
         gk_out[g * grad_per_head : (g + 1) * grad_per_head] = part.reshape(
             grad_per_head, grad_rows, hd
         )
@@ -330,7 +332,6 @@
         return copy(g_fin, g_res.at[s], g_send.at[d], g_recv.at[s], d)
 
     peers(lambda p: guarded(p, grad_pieces, lambda: k_copy(p, me).start()))
-    head_mates(lambda p: e_copy(p, my_head).start())
 
     def reduce_grads():
         gq_in[me] = gq_out[me]
@@ -349,6 +350,7 @@
     entries = n * rows * heads * heads_axis * hd
     err_ref[...] = jnp.sum(e_in[...], axis=0) / entries
     head_mates(lambda p: e_copy(p, my_head).wait_send())
+    peers(lambda p: n_copy(p, me).wait_send())
     x_copy(level).wait_send()
     c_copy(level).wait_send()
     loop(level + 1, levels, lambda up: z_copy(up).wait_send())
@@ -366,8 +368,8 @@
     peers(lambda s: guarded(s, grad_pieces, lambda: g_copy(0, s).wait_recv()))
     for g in range(heads):
         both = g_res[g * grad_per_head : (g + 1) * grad_per_head].astype(F32)
-        gq_ref[g] = both[:, :grad_rows].reshape(feat, hd).T
-        gk_ref[g] = both[:, grad_rows:].reshape(feat, hd).T
+        gq_ref[g] = both[:, :grad_rows].reshape(feat, hd)
+        gk_ref[g] = both[:, grad_rows:].reshape(feat, hd)
     guarded(me, grad_pieces, lambda: peers(lambda d: g_copy(d, me).wait_send()))
 
 
@@ -380,7 +382,7 @@
     state_pieces = min(n, heads * feat2 // 16)
     grad_pieces = min(n, heads * feat // 16)
     dims = (n, heads_axis, rows, heads, hd, feat, state_pieces, grad_pieces)
-    piece = heads * feat2 // state_pieces + 16
+    piece = heads * feat2 // state_pieces
     grad_rows = heads * feat // grad_pieces
     levels = n // PLANE
     dma = pltpu.SemaphoreType.DMA
@@ -389,15 +391,25 @@
         functools.partial(kernel, dims),
         out_shape=(
             jax.ShapeDtypeStruct((rows, heads * hd), BF16),
-            jax.ShapeDtypeStruct((heads, hd, feat), F32),
-            jax.ShapeDtypeStruct((heads, hd, feat), F32),
+            jax.ShapeDtypeStruct((heads, feat, hd), F32),
+            jax.ShapeDtypeStruct((heads, feat, hd), F32),
             jax.ShapeDtypeStruct((8, hd), F32),
         ),
-        in_specs=[vmem] * 5,
+        in_specs=[pl.BlockSpec(memory_space=pl.ANY)] * 5,
         out_specs=(vmem,) * 4,
         scratch_shapes=[
+            pltpu.VMEM((rows, heads * hd), BF16),
+            pltpu.VMEM((rows, hd), BF16),
+            pltpu.VMEM((heads, feat, hd), BF16),
+            pltpu.VMEM((heads, feat, hd), BF16),
+            dma((5,)),
+            pltpu.VMEM((heads, hd, rows), F32),
+            pltpu.VMEM((heads, 1, rows), F32),
+            pltpu.VMEM((16, hd), BF16),
+            pltpu.VMEM((n, 16, hd), BF16),
+            dma((n,)),
+            dma((n,)),
             pltpu.VMEM((n, 2, rows, hd), BF16),
-            pltpu.VMEM((heads * feat, hd), BF16),
             pltpu.VMEM((heads * rows, hd), BF16),
             pltpu.VMEM((heads, 1, rows), F32),
             pltpu.VMEM((heads, 1, rows), F32),
@@ -437,11 +449,9 @@
             dma((heads_axis,)),
             dma((heads_axis,)),
         ],
-        compiler_params=pltpu.CompilerParams(
-            collective_id=0, has_side_effects=True, vmem_limit_bytes=40 * 1024 * 1024
-        ),
-    )(queries, keys, values, feat_q, feat_k)
-    return student, grad_q, grad_k, error[0, 0]
+        compiler_params=pltpu.CompilerParams(collective_id=0, has_side_effects=True),
+    )(queries, keys, values, feat_q.swapaxes(1, 2), feat_k.swapaxes(1, 2))
+    return student, grad_q.swapaxes(1, 2), grad_k.swapaxes(1, 2), error[0, 0]
 
 
 def solution(mesh):

time: 53.2 us -> 52.6 us (0.989)
    unnamed x13 -> x7, local copies, waits for them, and re-layouts: 4.08 us -> 3.21 us
    slice x1, local copies, waits for them, and re-layouts: 0.51 us -> 1.2 us  [on_device(): return (student, grad_q.swapaxes(1, 2), grad_k.swapaxes(1, 2), error[0, 0])]
where the time goes in v2:
time: 52.6 us; the launch traced here: 52.4 us
  Pallas kernels  47.4 us (90%)
  local copies, waits for them, and re-layouts  4.41 us (8%)
  between operations  0.64 us (1%)
    pallas_call x1, Pallas kernels, on_device(): pl.pallas_call(functools.partial(kernel, dims), out_shape=(jax.ShapeDtype...  47.4 us
    unnamed x7, local copies, waits for them, and re-layouts  3.21 us
    slice x1, local copies, waits for them, and re-layouts, on_device(): return (student, grad_q.swapaxes(1, 2), grad_k.swapaxes(1, 2), error[0, 0])  1.2 us

profile of v2, /device:TPU:0, one launch (start us, length us, event | category | flops | bytes accessed | tf_op | source)
XLA Modules:
  0.0 52.4 jit_solution(7108530133339748899)
XLA Ops:
  0.6 47.4 %shard_map.84 = (bf16[128,512]{1,0:T(8,128)(2,1)}, f32[4,64,128]{2,1,0:T(8,128)}, f32[4,64,128]{2,1,0:T(8,128)}, f32[8,128]{1,0:T(8,128)}) custom-call(bf16[128,512]{1,0:T(8,128)(2,1)} %q_any.1, bf16[128,128]{1,0:T(8,128)(2,1)} %k_any.1, bf16[128,128]{1,0:T(8,128)(2,1)} %v_any.1, bf16[4,64,128]{2,1,0:T(8,128)(2,1)} %bitcast.7, bf16[4,64,128]{2,1,0:T(8,128)(2,1)} %bitcast.8), custom_call_target="tpu_custom_call" | custom-call | tf_op jit(solution)/shard_map/pallas_call | solution.py:390
  48.0 1.2 %slice.3 = f32[1,1]{1,0:T(1,128)} slice(f32[8,128]{1,0:T(8,128)} %get-tuple-element.11), slice={[0:1], [0:1]} | slice | bytes 8 | tf_op jit(solution)/shard_map/slice | solution.py:454
  49.2 0.0 copy-start.1
  49.2 1.6 %copy.12 = bf16[128,512]{1,0:T(8,128)(2,1)} copy(bf16[128,512]{1,0:T(8,128)(2,1)} %get-tuple-element.16) | data formatting | bytes 262144
  50.8 0.0 copy-done.1
  50.8 0.0 copy-start
  50.8 0.7 %copy.13 = f32[4,128,64]{1,2,0:T(8,128)} copy(f32[4,128,64]{1,2,0:T(8,128)S(1)} %bitcast.6) | data formatting | bytes 262144
  51.5 0.3 copy-done
  51.8 0.7 %copy.14 = f32[4,128,64]{1,2,0:T(8,128)} copy(f32[4,128,64]{1,2,0:T(8,128)S(1)} %bitcast.5) | data formatting | bytes 262144
Async XLA Ops:
  49.2 1.6 %copy-start.1 = (f32[4,64,128]{2,1,0:T(8,128)S(1)}, f32[4,64,128]{2,1,0:T(8,128)}, u32[]{:S(2)}) copy-start(f32[4,64,128]{2,1,0:T(8,128)} %get-tuple-element.9) | copy-start | bytes 393220
  50.8 1.0 %copy-start = (f32[4,64,128]{2,1,0:T(8,128)S(1)}, f32[4,64,128]{2,1,0:T(8,128)}, u32[]{:S(2)}) copy-start(f32[4,64,128]{2,1,0:T(8,128)} %get-tuple-element.10) | copy-start | bytes 393220

commit v3 on v2

--- a/solution.py
+++ b/solution.py
@@ -50,11 +50,11 @@
     dims,
     q_any, k_any, v_any, fq_any, fk_any,
     student_ref, gq_ref, gk_ref, err_ref,
-    q_ref, v_ref, fq_ref, fk_ref, in_sem, numl, denl, x_out, x_in, n_send, n_recv,
+    q_ref, v_ref, fq_ref, fk_ref, in_sem, numl, denl,
     kv, qs, top, total, acc, s_t, s_n, fqp, fkp, dfq, ldfk,
-    st_out, st_in, st_fin, st_res, gq_out, gq_in, gk_out, gk_in, g_fin, g_res, e_out, e_in,
+    st_out, st_in, st_fin, st_res, g_out, g_in, g_fin, g_res, e_out, e_in,
     z_send, x_send, c_send, kv_recv, a_send, a_recv, b_send, b_recv,
-    q_send, q_recv, k_send, k_recv, g_send, g_recv, e_send, e_recv,
+    k_send, k_recv, g_send, g_recv, e_send, e_recv,
 ):
     n, heads_axis, rows, heads, hd, feat, state_pieces, grad_pieces = dims
     me = lax.axis_index("ctx")
@@ -74,17 +74,20 @@
         )
 
     def peers(body):
+        if n <= 16:
+            for k in range(1, n):
+                body(lax.rem(me + k, n))
+            return
+
         def step(k, carry):
-            body((me + k) % n)
+            body(lax.rem(me + k, n))
             return carry
 
         lax.fori_loop(1, n, step, 0)
 
-    def guarded(index, pieces, body):
-        if pieces == n:
-            body()
-        else:
-            pl.when(index < pieces)(body)
+    def whole(ref, send, recv):
+        part = ref.at[pl.ds(0, n - 1)]
+        return copy(part, part, send, recv, core_mate)
 
     def head_mates(body):
         def step(k, carry):
@@ -238,7 +241,7 @@
         dnb = dnumer.astype(BF16)
         dmat = jnp.where(causal, dot(values, dnb) + dden, 0.0).astype(BF16)
         state = dot_nt(fq_t, dnb).astype(BF16)
-        st_out[g * per_head : (g + 1) * per_head] = state.reshape(per_head, piece, hd)
+        st_out[g * per_head : (g + 1) * per_head, :piece, :] = state.reshape(per_head, piece, hd)
         d_high, d_low = split(jnp.broadcast_to(dden, (16, rows)))
         norm_rows.append(dot_nt(d_high, fq_t) + dot_nt(d_low, fq_t))
         high, low = split(s_n[g * feat2 : (g + 1) * feat2, :hd])
@@ -253,51 +256,44 @@
     extra = jnp.where(extra_row < 12, first, error - first)
     for g in range(heads):
         extra = jnp.where(extra_row == g, norm_rows[g], extra)
-    x_out[...] = extra.astype(BF16)
-
-    def n_copy(p, s):
-        return copy(x_out, x_in.at[s], n_send.at[p], n_recv.at[s], p)
-
-    def a_copy(p, s):
-        return copy(st_out.at[p], st_in.at[s], a_send.at[p], a_recv.at[s], p)
-
-    peers(lambda p: guarded(p, state_pieces, lambda: a_copy(p, me).start()))
-    peers(lambda p: n_copy(p, me).start())
+    extra = extra.astype(BF16)
+    for p in range(n):
+        st_out[p, piece:, :] = extra
+        if p >= state_pieces:
+            st_out[p, :piece, :] = jnp.zeros((piece, hd), BF16)
+
+    def a_copy(p):
+        return copy(st_out.at[p], st_in.at[me], a_send, a_recv, p)
+
+    peers(lambda p: a_copy(p).start())
+    st_in[me] = st_out[me]
 
     grad_rows = heads * feat // grad_pieces
     grad_per_head = grad_pieces // heads
     for g in range(heads):
         dlq = feature_grad(fqp[g], dfq[g]).astype(BF16)
         part = dot(dlq, qs[g * rows : (g + 1) * rows, :]).astype(BF16)
-        gq_out[g * grad_per_head : (g + 1) * grad_per_head] = part.reshape(
+        g_out[g * grad_per_head : (g + 1) * grad_per_head, :grad_rows, :] = part.reshape(
             grad_per_head, grad_rows, hd
         )
-
-    def q_copy(p, s):
-        return copy(gq_out.at[p], gq_in.at[s], q_send.at[p], q_recv.at[s], p)
-
-    def b_copy(d, s):
-        return copy(st_fin.at[d], st_res.at[s], b_send.at[d], b_recv.at[s], d)
-
-    def reduce_states():
-        st_in[me] = st_out[me]
-        peers(lambda s: a_copy(0, s).wait_recv())
-
-        def suffix(t, states):
-            d = n - 1 - t
-            st_fin[d] = states.astype(BF16)
-            return states + st_in[d].astype(F32)
-
-        lax.fori_loop(0, n, suffix, jnp.zeros((piece, hd), F32))
-        peers(lambda d: b_copy(d, me).start())
-        st_res[me] = st_fin[me]
-
-    guarded(me, state_pieces, reduce_states)
-    peers(lambda p: guarded(p, grad_pieces, lambda: q_copy(p, me).start()))
-
-    x_in[me] = x_out[...]
-    peers(lambda s: n_copy(0, s).wait_recv())
-    extras = x_in[...].astype(F32)
+    for p in range(grad_pieces, n):
+        g_out[p] = jnp.zeros((2 * grad_rows, hd), BF16)
+
+    def b_copy(d):
+        return copy(st_fin.at[d], st_res.at[me], b_send, b_recv, d)
+
+    whole(st_in, a_send, a_recv).wait_recv()
+
+    def suffix(t, states):
+        d = n - 1 - t
+        st_fin[d] = states.astype(BF16)
+        return states + st_in[d, :piece, :].astype(F32)
+
+    lax.fori_loop(0, n, suffix, jnp.zeros((piece, hd), F32), unroll=n <= 16)
+    peers(lambda d: b_copy(d).start())
+    st_res[me] = st_fin[me]
+
+    extras = st_in[:, piece:, :].astype(F32)
     later_norms = jnp.sum(
         jnp.where(lax.broadcasted_iota(jnp.int32, extras.shape, 0) > me, extras, 0.0), axis=0
     )
@@ -315,42 +311,34 @@
         norm = jnp.broadcast_to(later_norms[g : g + 1], (rows, feat2)).T
         ldfk[g] += norm
 
-    peers(lambda s: guarded(s, state_pieces, lambda: b_copy(0, s).wait_recv()))
+    whole(st_res, b_send, b_recv).wait_recv()
     for g in range(heads):
         later = st_res[g * per_head : (g + 1) * per_head].reshape(feat2, hd)
         dfk = ldfk[g] + dot(later, v_t)
         dlk = feature_grad(fkp[g], dfk).astype(BF16)
         part = dot(dlk, kv[me, 0]).astype(BF16)
-        gk_out[g * grad_per_head : (g + 1) * grad_per_head] = part.reshape(
+        g_out[g * grad_per_head : (g + 1) * grad_per_head, grad_rows:, :] = part.reshape(
             grad_per_head, grad_rows, hd
         )
 
-    def k_copy(p, s):
-        return copy(gk_out.at[p], gk_in.at[s], k_send.at[p], k_recv.at[s], p)
-
-    def g_copy(d, s):
-        return copy(g_fin, g_res.at[s], g_send.at[d], g_recv.at[s], d)
-
-    peers(lambda p: guarded(p, grad_pieces, lambda: k_copy(p, me).start()))
-
-    def reduce_grads():
-        gq_in[me] = gq_out[me]
-        gk_in[me] = gk_out[me]
-        peers(lambda s: q_copy(0, s).wait_recv())
-        g_fin[:grad_rows] = jnp.sum(gq_in[...].astype(F32), axis=0).astype(BF16)
-        peers(lambda s: k_copy(0, s).wait_recv())
-        g_fin[grad_rows:] = jnp.sum(gk_in[...].astype(F32), axis=0).astype(BF16)
-        peers(lambda d: g_copy(d, me).start())
-        g_res[me] = g_fin[...]
-
-    guarded(me, grad_pieces, reduce_grads)
+    def k_copy(p):
+        return copy(g_out.at[p], g_in.at[me], k_send, k_recv, p)
+
+    def g_copy(d):
+        return copy(g_fin, g_res.at[me], g_send, g_recv, d)
+
+    peers(lambda p: k_copy(p).start())
+    g_in[me] = g_out[me]
+    whole(g_in, k_send, k_recv).wait_recv()
+    g_fin[...] = jnp.sum(g_in[...].astype(F32), axis=0).astype(BF16)
+    peers(lambda d: g_copy(d).start())
+    g_res[me] = g_fin[...]
 
     e_in[my_head] = e_out[...]
     head_mates(lambda s: e_copy(0, s).wait_recv())
     entries = n * rows * heads * heads_axis * hd
     err_ref[...] = jnp.sum(e_in[...], axis=0) / entries
     head_mates(lambda p: e_copy(p, my_head).wait_send())
-    peers(lambda p: n_copy(p, me).wait_send())
     x_copy(level).wait_send()
     c_copy(level).wait_send()
     loop(level + 1, levels, lambda up: z_copy(up).wait_send())
@@ -361,16 +349,15 @@
 
     loop(0, level, relay_end)
     loop(0, level + 1, lambda t: f_copy(t).wait_send())
-    peers(lambda p: guarded(p, state_pieces, lambda: a_copy(p, me).wait_send()))
-    guarded(me, state_pieces, lambda: peers(lambda d: b_copy(d, me).wait_send()))
-    peers(lambda p: guarded(p, grad_pieces, lambda: q_copy(p, me).wait_send()))
-    peers(lambda p: guarded(p, grad_pieces, lambda: k_copy(p, me).wait_send()))
-    peers(lambda s: guarded(s, grad_pieces, lambda: g_copy(0, s).wait_recv()))
+    whole(st_in, a_send, a_recv).wait_send()
+    whole(st_res, b_send, b_recv).wait_send()
+    whole(g_in, k_send, k_recv).wait_send()
+    whole(g_res, g_send, g_recv).wait_recv()
     for g in range(heads):
         both = g_res[g * grad_per_head : (g + 1) * grad_per_head].astype(F32)
         gq_ref[g] = both[:, :grad_rows].reshape(feat, hd)
         gk_ref[g] = both[:, grad_rows:].reshape(feat, hd)
-    guarded(me, grad_pieces, lambda: peers(lambda d: g_copy(d, me).wait_send()))
+    whole(g_res, g_send, g_recv).wait_send()
 
 
 def on_device(queries, keys, values, feat_q, feat_k):
@@ -395,7 +382,7 @@
             jax.ShapeDtypeStruct((heads, feat, hd), F32),
             jax.ShapeDtypeStruct((8, hd), F32),
         ),
-        in_specs=[pl.BlockSpec(memory_space=pl.ANY)] * 5,
+        in_specs=[pl.BlockSpec(memory_space=pltpu.HBM)] * 5,
         out_specs=(vmem,) * 4,
         scratch_shapes=[
             pltpu.VMEM((rows, heads * hd), BF16),
@@ -405,10 +392,6 @@
             dma((5,)),
             pltpu.VMEM((heads, hd, rows), F32),
             pltpu.VMEM((heads, 1, rows), F32),
-            pltpu.VMEM((16, hd), BF16),
-            pltpu.VMEM((n, 16, hd), BF16),
-            dma((n,)),
-            dma((n,)),
             pltpu.VMEM((n, 2, rows, hd), BF16),
             pltpu.VMEM((heads * rows, hd), BF16),
             pltpu.VMEM((heads, 1, rows), F32),
@@ -420,36 +403,34 @@
             pltpu.VMEM((heads, feat2, rows), F32),
             pltpu.VMEM((heads, feat2, rows), F32),
             pltpu.VMEM((heads, feat2, rows), F32),
-            pltpu.VMEM((state_pieces, piece, hd), BF16),
+            pltpu.VMEM((n, piece + 16, hd), BF16),
+            pltpu.VMEM((n, piece + 16, hd), BF16),
             pltpu.VMEM((n, piece, hd), BF16),
             pltpu.VMEM((n, piece, hd), BF16),
-            pltpu.VMEM((state_pieces, piece, hd), BF16),
-            pltpu.VMEM((grad_pieces, grad_rows, hd), BF16),
-            pltpu.VMEM((n, grad_rows, hd), BF16),
-            pltpu.VMEM((grad_pieces, grad_rows, hd), BF16),
-            pltpu.VMEM((n, grad_rows, hd), BF16),
+            pltpu.VMEM((n, 2 * grad_rows, hd), BF16),
+            pltpu.VMEM((n, 2 * grad_rows, hd), BF16),
             pltpu.VMEM((2 * grad_rows, hd), BF16),
-            pltpu.VMEM((grad_pieces, 2 * grad_rows, hd), BF16),
+            pltpu.VMEM((n, 2 * grad_rows, hd), BF16),
             pltpu.VMEM((8, hd), F32),
             pltpu.VMEM((heads_axis, 8, hd), F32),
             dma((levels,)),
             dma((levels,)),
             dma((2, levels)),
             dma((n,)),
-            dma((n,)),
-            dma((n,)),
-            dma((n,)),
-            dma((n,)),
-            dma((n,)),
-            dma((n,)),
-            dma((n,)),
-            dma((n,)),
-            dma((n,)),
-            dma((n,)),
+            dma(()),
+            dma(()),
+            dma(()),
+            dma(()),
+            dma(()),
+            dma(()),
+            dma(()),
+            dma(()),
             dma((heads_axis,)),
             dma((heads_axis,)),
         ],
-        compiler_params=pltpu.CompilerParams(collective_id=0, has_side_effects=True),
+        compiler_params=pltpu.CompilerParams(
+            collective_id=0, has_side_effects=True, vmem_limit_bytes=40 * 1024 * 1024
+        ),
     )(queries, keys, values, feat_q.swapaxes(1, 2), feat_k.swapaxes(1, 2))
     return student, grad_q.swapaxes(1, 2), grad_k.swapaxes(1, 2), error[0, 0]
 

time: 52.6 us -> 52.8 us (level)
  Pallas kernels: 47.4 us -> 45.2 us
  local copies, waits for them, and re-layouts: 4.41 us -> 6.57 us
    unnamed x7 -> x13, local copies, waits for them, and re-layouts: 3.21 us -> 6.05 us
    pallas_call x1, Pallas kernels: 47.4 us -> 45.2 us  [on_device(): pl.pallas_call(functools.partial(kernel, dims), out_shape=(jax.ShapeDtype...]
    slice x1, local copies, waits for them, and re-layouts: 1.2 us -> 0.51 us  [on_device(): return (student, grad_q.swapaxes(1, 2), grad_k.swapaxes(1, 2), error[0, 0])]
where the time goes in v3:
time: 52.8 us; the launch traced here: 52.4 us
  Pallas kernels  45.2 us (86%)
  local copies, waits for them, and re-layouts  6.57 us (12%)
  between operations  0.65 us (1%)
    pallas_call x1, Pallas kernels, on_device(): pl.pallas_call(functools.partial(kernel, dims), out_shape=(jax.ShapeDtype...  45.2 us
    unnamed x13, local copies, waits for them, and re-layouts  6.05 us

profile of v3, /device:TPU:0, one launch (start us, length us, event | category | flops | bytes accessed | tf_op | source)
XLA Modules:
  0.0 52.4 jit_solution(8208206618842105507)
XLA Ops:
  0.6 0.0 copy-start
  0.6 0.9 %copy-done = bf16[128,512]{1,0:T(8,128)(2,1)S(1)} copy-done((bf16[128,512]{1,0:T(8,128)(2,1)S(1)}, bf16[128,512]{1,0:T(8,128)(2,1)}, u32[]{:S(2)}) %copy-start) | copy-done | bytes 131096
  1.5 0.0 copy-start.1
  1.5 0.8 %copy-done.1 = bf16[4,128,64]{1,2,0:T(8,128)(2,1)S(1)} copy-done((bf16[4,128,64]{1,2,0:T(8,128)(2,1)S(1)}, bf16[4,128,64]{1,2,0:T(8,128)(2,1)}, u32[]{:S(2)}) %copy-start.1) | copy-done | bytes 65560
  2.4 0.0 copy-start.2
  2.4 0.8 %copy-done.2 = bf16[4,128,64]{1,2,0:T(8,128)(2,1)S(1)} copy-done((bf16[4,128,64]{1,2,0:T(8,128)(2,1)S(1)}, bf16[4,128,64]{1,2,0:T(8,128)(2,1)}, u32[]{:S(2)}) %copy-start.2) | copy-done | bytes 65560
  3.2 0.0 copy-start.3
  3.2 0.8 %copy-done.3 = bf16[128,128]{1,0:T(8,128)(2,1)S(1)} copy-done((bf16[128,128]{1,0:T(8,128)(2,1)S(1)}, bf16[128,128]{1,0:T(8,128)(2,1)}, u32[]{:S(2)}) %copy-start.3) | copy-done | bytes 32792
  4.0 0.0 copy-start.4
  4.0 0.8 %copy-done.4 = bf16[128,128]{1,0:T(8,128)(2,1)S(1)} copy-done((bf16[128,128]{1,0:T(8,128)(2,1)S(1)}, bf16[128,128]{1,0:T(8,128)(2,1)}, u32[]{:S(2)}) %copy-start.4) | copy-done | bytes 32792
  4.7 45.2 %shard_map.84 = (bf16[128,512]{1,0:T(8,128)(2,1)S(1)}, f32[4,64,128]{2,1,0:T(8,128)S(1)}, f32[4,64,128]{2,1,0:T(8,128)S(1)}, f32[8,128]{1,0:T(8,128)S(1)}) custom-call(bf16[128,512]{1,0:T(8,128)(2,1)S(1)} %copy-done, bf16[128,128]{1,0:T(8,128)(2,1)S(1)} %copy-done.3, bf16[128,128]{1,0:T(8,128)(2,1)S(1)} %copy-done.4, bf16[4,64,128]{2,1,0:T(8,128)(2,1)S(1)} %bitcast.7, ...), custom_call_target="tpu_custom_call" | custom-call | tf_op jit(solution)/shard_map/pallas_call | solution.py:377
  49.9 0.5 slice.3
  50.4 0.7 %copy.12 = bf16[128,512]{1,0:T(8,128)(2,1)} copy(bf16[128,512]{1,0:T(8,128)(2,1)S(1)} %get-tuple-element.16) | data formatting | bytes 262144
  51.1 0.7 %copy.13 = f32[4,128,64]{1,2,0:T(8,128)} copy(f32[4,128,64]{1,2,0:T(8,128)S(1)} %bitcast.6) | data formatting | bytes 262144
  51.7 0.7 %copy.14 = f32[4,128,64]{1,2,0:T(8,128)} copy(f32[4,128,64]{1,2,0:T(8,128)S(1)} %bitcast.5) | data formatting | bytes 262144
Async XLA Ops:
  0.6 0.9 %copy-start = (bf16[128,512]{1,0:T(8,128)(2,1)S(1)}, bf16[128,512]{1,0:T(8,128)(2,1)}, u32[]{:S(2)}) copy-start(bf16[128,512]{1,0:T(8,128)(2,1)} %q_any.1) | copy-start | bytes 393220
  1.5 0.8 %copy-start.1 = (bf16[4,128,64]{1,2,0:T(8,128)(2,1)S(1)}, bf16[4,128,64]{1,2,0:T(8,128)(2,1)}, u32[]{:S(2)}) copy-start(bf16[4,128,64]{1,2,0:T(8,128)(2,1)} %param.8) | copy-start | bytes 196612
  2.4 0.8 %copy-start.2 = (bf16[4,128,64]{1,2,0:T(8,128)(2,1)S(1)}, bf16[4,128,64]{1,2,0:T(8,128)(2,1)}, u32[]{:S(2)}) copy-start(bf16[4,128,64]{1,2,0:T(8,128)(2,1)} %param.9) | copy-start | bytes 196612
  3.2 0.8 %copy-start.3 = (bf16[128,128]{1,0:T(8,128)(2,1)S(1)}, bf16[128,128]{1,0:T(8,128)(2,1)}, u32[]{:S(2)}) copy-start(bf16[128,128]{1,0:T(8,128)(2,1)} %k_any.1) | copy-start | bytes 98308
  4.0 0.8 %copy-start.4 = (bf16[128,128]{1,0:T(8,128)(2,1)S(1)}, bf16[128,128]{1,0:T(8,128)(2,1)}, u32[]{:S(2)}) copy-start(bf16[128,128]{1,0:T(8,128)(2,1)} %v_any.1) | copy-start | bytes 98308

commit v4 on v3

--- a/solution.py
+++ b/solution.py
@@ -48,11 +48,11 @@
 
 def kernel(
     dims,
-    q_any, k_any, v_any, fq_any, fk_any,
+    q_ref, k_ref, v_ref, fq_ref, fk_ref,
     student_ref, gq_ref, gk_ref, err_ref,
-    q_ref, v_ref, fq_ref, fk_ref, in_sem, numl, denl,
+    numl, denl, x_out, x_in, n_send, n_recv, q_send, q_recv,
     kv, qs, top, total, acc, s_t, s_n, fqp, fkp, dfq, ldfk,
-    st_out, st_in, st_fin, st_res, g_out, g_in, g_fin, g_res, e_out, e_in,
+    st_out, st_in, st_fin, st_res, gq_out, gq_in, gk_out, gk_in, g_fin, g_res, e_out, e_in,
     z_send, x_send, c_send, kv_recv, a_send, a_recv, b_send, b_recv,
     k_send, k_recv, g_send, g_recv, e_send, e_recv,
 ):
@@ -96,20 +96,10 @@
 
         lax.fori_loop(1, heads_axis, step, 0)
 
-    loads = [
-        pltpu.make_async_copy(src, dst, in_sem.at[i])
-        for i, (src, dst) in enumerate(
-            ((k_any, kv.at[me, 0]), (v_any, v_ref), (fk_any, fk_ref), (q_any, q_ref), (fq_any, fq_ref))
-        )
-    ]
-    for load in loads:
-        load.start()
-
     barrier = pltpu.get_barrier_semaphore()
     peers(lambda p: pl.semaphore_signal(barrier, inc=1, device_id=(p, my_head), device_id_type=MESH))
     head_mates(lambda p: pl.semaphore_signal(barrier, inc=1, device_id=(me, p), device_id_type=MESH))
-    loads[0].wait()
-    loads[1].wait()
+    kv[me, 0] = k_ref[...]
     v_t = v_ref[...].astype(F32).T.astype(BF16)
     kv[me, 1] = v_t
     pl.semaphore_wait(barrier, n - 1 + heads_axis - 1)
@@ -146,11 +136,9 @@
     key_row = lax.broadcasted_iota(jnp.int32, (rows, rows), 0)
     query_col = lax.broadcasted_iota(jnp.int32, (rows, rows), 1)
     causal = key_row <= query_col
-    for load in loads[2:]:
-        load.wait()
     w_k = fk_ref[...].reshape(heads * feat, hd)
     w_q = fq_ref[...].reshape(heads * feat, hd)
-    own_k = dot_nt(w_k, kv[me, 0])
+    own_k = dot_nt(w_k, k_ref[...])
     for g in range(heads):
         q_g = q_ref[:, g * hd : (g + 1) * hd]
         qs[g * rows : (g + 1) * rows, :] = q_g
@@ -221,9 +209,21 @@
     per_head = state_pieces // heads
     piece = heads * feat2 // state_pieces
     squares = jnp.zeros((hd, rows), F32)
-    norm_rows = []
+    norm_rows = {}
+    order = [*range(0, heads, 2), *range(1, heads, 2)]
+
+    def a_copy(p):
+        return copy(st_out.at[p], st_in.at[me], a_send, a_recv, p)
+
+    def to_others(targets, start):
+        for p in targets:
+            pl.when(me != p)(lambda p=p: start(p).start())
+
     values = v_ref[...]
-    for g in range(heads):
+    for p in range(state_pieces, n):
+        st_out[p] = jnp.zeros((piece, hd), BF16)
+    to_others(range(state_pieces, n), a_copy)
+    for g in order:
         fq_t = fqp[g].astype(BF16)
         fk_t = fkp[g].astype(BF16)
         high, low = split(s_t[:, g * feat2 : (g + 1) * feat2])
@@ -241,9 +241,11 @@
         dnb = dnumer.astype(BF16)
         dmat = jnp.where(causal, dot(values, dnb) + dden, 0.0).astype(BF16)
         state = dot_nt(fq_t, dnb).astype(BF16)
-        st_out[g * per_head : (g + 1) * per_head, :piece, :] = state.reshape(per_head, piece, hd)
+        for j in range(per_head):
+            st_out[j * heads + g] = state[j * piece : (j + 1) * piece]
+        to_others(range(g, state_pieces, heads), a_copy)
         d_high, d_low = split(jnp.broadcast_to(dden, (16, rows)))
-        norm_rows.append(dot_nt(d_high, fq_t) + dot_nt(d_low, fq_t))
+        norm_rows[g] = dot_nt(d_high, fq_t) + dot_nt(d_low, fq_t)
         high, low = split(s_n[g * feat2 : (g + 1) * feat2, :hd])
         dfq[g] = (
             dot(jnp.concatenate([fk_t, high, low], axis=1), jnp.concatenate([dmat, dnb, dnb], axis=0))
@@ -256,28 +258,31 @@
     extra = jnp.where(extra_row < 12, first, error - first)
     for g in range(heads):
         extra = jnp.where(extra_row == g, norm_rows[g], extra)
-    extra = extra.astype(BF16)
-    for p in range(n):
-        st_out[p, piece:, :] = extra
-        if p >= state_pieces:
-            st_out[p, :piece, :] = jnp.zeros((piece, hd), BF16)
-
-    def a_copy(p):
-        return copy(st_out.at[p], st_in.at[me], a_send, a_recv, p)
-
-    peers(lambda p: a_copy(p).start())
+    x_out[...] = extra.astype(BF16)
+
+    def n_copy(p):
+        return copy(x_out, x_in.at[me], n_send, n_recv, p)
+
+    peers(lambda p: n_copy(p).start())
     st_in[me] = st_out[me]
+    x_in[me] = x_out[...]
 
     grad_rows = heads * feat // grad_pieces
     grad_per_head = grad_pieces // heads
     for g in range(heads):
         dlq = feature_grad(fqp[g], dfq[g]).astype(BF16)
         part = dot(dlq, qs[g * rows : (g + 1) * rows, :]).astype(BF16)
-        g_out[g * grad_per_head : (g + 1) * grad_per_head, :grad_rows, :] = part.reshape(
-            grad_per_head, grad_rows, hd
-        )
+        for j in range(grad_per_head):
+            gq_out[j * heads + g] = part[j * grad_rows : (j + 1) * grad_rows]
     for p in range(grad_pieces, n):
-        g_out[p] = jnp.zeros((2 * grad_rows, hd), BF16)
+        gq_out[p] = jnp.zeros((grad_rows, hd), BF16)
+        gk_out[p] = jnp.zeros((grad_rows, hd), BF16)
+
+    def q_copy(p):
+        return copy(gq_out.at[p], gq_in.at[me], q_send, q_recv, p)
+
+    def k_copy(p):
+        return copy(gk_out.at[p], gk_in.at[me], k_send, k_recv, p)
 
     def b_copy(d):
         return copy(st_fin.at[d], st_res.at[me], b_send, b_recv, d)
@@ -287,13 +292,17 @@
     def suffix(t, states):
         d = n - 1 - t
         st_fin[d] = states.astype(BF16)
-        return states + st_in[d, :piece, :].astype(F32)
+        return states + st_in[d].astype(F32)
 
     lax.fori_loop(0, n, suffix, jnp.zeros((piece, hd), F32), unroll=n <= 16)
     peers(lambda d: b_copy(d).start())
+    peers(lambda p: q_copy(p).start())
+    to_others(range(grad_pieces, n), k_copy)
+    gq_in[me] = gq_out[me]
     st_res[me] = st_fin[me]
 
-    extras = st_in[:, piece:, :].astype(F32)
+    whole(x_in, n_send, n_recv).wait_recv()
+    extras = x_in[...].astype(F32)
     later_norms = jnp.sum(
         jnp.where(lax.broadcasted_iota(jnp.int32, extras.shape, 0) > me, extras, 0.0), axis=0
     )
@@ -312,25 +321,23 @@
         ldfk[g] += norm
 
     whole(st_res, b_send, b_recv).wait_recv()
-    for g in range(heads):
-        later = st_res[g * per_head : (g + 1) * per_head].reshape(feat2, hd)
+    for g in order:
+        later = jnp.concatenate([st_res[j * heads + g] for j in range(per_head)], axis=0)
         dfk = ldfk[g] + dot(later, v_t)
         dlk = feature_grad(fkp[g], dfk).astype(BF16)
-        part = dot(dlk, kv[me, 0]).astype(BF16)
-        g_out[g * grad_per_head : (g + 1) * grad_per_head, grad_rows:, :] = part.reshape(
-            grad_per_head, grad_rows, hd
-        )
-
-    def k_copy(p):
-        return copy(g_out.at[p], g_in.at[me], k_send, k_recv, p)
+        part = dot(dlk, k_ref[...]).astype(BF16)
+        for j in range(grad_per_head):
+            gk_out[j * heads + g] = part[j * grad_rows : (j + 1) * grad_rows]
+        to_others(range(g, grad_pieces, heads), k_copy)
 
     def g_copy(d):
         return copy(g_fin, g_res.at[me], g_send, g_recv, d)
 
-    peers(lambda p: k_copy(p).start())
-    g_in[me] = g_out[me]
-    whole(g_in, k_send, k_recv).wait_recv()
-    g_fin[...] = jnp.sum(g_in[...].astype(F32), axis=0).astype(BF16)
+    gk_in[me] = gk_out[me]
+    whole(gq_in, q_send, q_recv).wait_recv()
+    g_fin[:grad_rows] = jnp.sum(gq_in[...].astype(F32), axis=0).astype(BF16)
+    whole(gk_in, k_send, k_recv).wait_recv()
+    g_fin[grad_rows:] = jnp.sum(gk_in[...].astype(F32), axis=0).astype(BF16)
     peers(lambda d: g_copy(d).start())
     g_res[me] = g_fin[...]
 
@@ -351,10 +358,12 @@
     loop(0, level + 1, lambda t: f_copy(t).wait_send())
     whole(st_in, a_send, a_recv).wait_send()
     whole(st_res, b_send, b_recv).wait_send()
-    whole(g_in, k_send, k_recv).wait_send()
+    whole(x_in, n_send, n_recv).wait_send()
+    whole(gq_in, q_send, q_recv).wait_send()
+    whole(gk_in, k_send, k_recv).wait_send()
     whole(g_res, g_send, g_recv).wait_recv()
     for g in range(heads):
-        both = g_res[g * grad_per_head : (g + 1) * grad_per_head].astype(F32)
+        both = jnp.stack([g_res[j * heads + g] for j in range(grad_per_head)]).astype(F32)
         gq_ref[g] = both[:, :grad_rows].reshape(feat, hd)
         gk_ref[g] = both[:, grad_rows:].reshape(feat, hd)
     whole(g_res, g_send, g_recv).wait_send()
@@ -382,16 +391,17 @@
             jax.ShapeDtypeStruct((heads, feat, hd), F32),
             jax.ShapeDtypeStruct((8, hd), F32),
         ),
-        in_specs=[pl.BlockSpec(memory_space=pltpu.HBM)] * 5,
+        in_specs=[vmem] * 5,
         out_specs=(vmem,) * 4,
         scratch_shapes=[
-            pltpu.VMEM((rows, heads * hd), BF16),
-            pltpu.VMEM((rows, hd), BF16),
-            pltpu.VMEM((heads, feat, hd), BF16),
-            pltpu.VMEM((heads, feat, hd), BF16),
-            dma((5,)),
             pltpu.VMEM((heads, hd, rows), F32),
             pltpu.VMEM((heads, 1, rows), F32),
+            pltpu.VMEM((16, hd), BF16),
+            pltpu.VMEM((n, 16, hd), BF16),
+            dma(()),
+            dma(()),
+            dma(()),
+            dma(()),
             pltpu.VMEM((n, 2, rows, hd), BF16),
             pltpu.VMEM((heads * rows, hd), BF16),
             pltpu.VMEM((heads, 1, rows), F32),
@@ -403,12 +413,14 @@
             pltpu.VMEM((heads, feat2, rows), F32),
             pltpu.VMEM((heads, feat2, rows), F32),
             pltpu.VMEM((heads, feat2, rows), F32),
-            pltpu.VMEM((n, piece + 16, hd), BF16),
-            pltpu.VMEM((n, piece + 16, hd), BF16),
             pltpu.VMEM((n, piece, hd), BF16),
             pltpu.VMEM((n, piece, hd), BF16),
-            pltpu.VMEM((n, 2 * grad_rows, hd), BF16),
-            pltpu.VMEM((n, 2 * grad_rows, hd), BF16),
+            pltpu.VMEM((n, piece, hd), BF16),
+            pltpu.VMEM((n, piece, hd), BF16),
+            pltpu.VMEM((n, grad_rows, hd), BF16),
+            pltpu.VMEM((n, grad_rows, hd), BF16),
+            pltpu.VMEM((n, grad_rows, hd), BF16),
+            pltpu.VMEM((n, grad_rows, hd), BF16),
             pltpu.VMEM((2 * grad_rows, hd), BF16),
             pltpu.VMEM((n, 2 * grad_rows, hd), BF16),
             pltpu.VMEM((8, hd), F32),

time: 52.8 us -> 50.5 us (0.956)
  Pallas kernels: 45.2 us -> 42.9 us
    pallas_call x1, Pallas kernels: 45.2 us -> 42.9 us  [on_device(): pl.pallas_call(functools.partial(kernel, dims), out_shape=(jax.ShapeDtype...]
where the time goes in v4:
time: 50.5 us; the launch traced here: 50.1 us
  Pallas kernels  42.9 us (85%)
  local copies, waits for them, and re-layouts  6.57 us (13%)
  between operations  0.65 us (1%)
    pallas_call x1, Pallas kernels, on_device(): pl.pallas_call(functools.partial(kernel, dims), out_shape=(jax.ShapeDtype...  42.9 us
    unnamed x13, local copies, waits for them, and re-layouts  6.05 us

profile of v4, /device:TPU:0, one launch (start us, length us, event | category | flops | bytes accessed | tf_op | source)
XLA Modules:
  0.0 50.1 jit_solution(13388999478708458036)
XLA Ops:
  0.6 0.0 copy-start
  0.6 0.9 %copy-done = bf16[128,512]{1,0:T(8,128)(2,1)S(1)} copy-done((bf16[128,512]{1,0:T(8,128)(2,1)S(1)}, bf16[128,512]{1,0:T(8,128)(2,1)}, u32[]{:S(2)}) %copy-start) | copy-done | bytes 131096
  1.5 0.0 copy-start.1
  1.5 0.8 %copy-done.1 = bf16[4,128,64]{1,2,0:T(8,128)(2,1)S(1)} copy-done((bf16[4,128,64]{1,2,0:T(8,128)(2,1)S(1)}, bf16[4,128,64]{1,2,0:T(8,128)(2,1)}, u32[]{:S(2)}) %copy-start.1) | copy-done | bytes 65560
  2.4 0.0 copy-start.2
  2.4 0.8 %copy-done.2 = bf16[4,128,64]{1,2,0:T(8,128)(2,1)S(1)} copy-done((bf16[4,128,64]{1,2,0:T(8,128)(2,1)S(1)}, bf16[4,128,64]{1,2,0:T(8,128)(2,1)}, u32[]{:S(2)}) %copy-start.2) | copy-done | bytes 65560
  3.2 0.0 copy-start.3
  3.2 0.8 %copy-done.3 = bf16[128,128]{1,0:T(8,128)(2,1)S(1)} copy-done((bf16[128,128]{1,0:T(8,128)(2,1)S(1)}, bf16[128,128]{1,0:T(8,128)(2,1)}, u32[]{:S(2)}) %copy-start.3) | copy-done | bytes 32792
  4.0 0.0 copy-start.4
  4.0 0.8 %copy-done.4 = bf16[128,128]{1,0:T(8,128)(2,1)S(1)} copy-done((bf16[128,128]{1,0:T(8,128)(2,1)S(1)}, bf16[128,128]{1,0:T(8,128)(2,1)}, u32[]{:S(2)}) %copy-start.4) | copy-done | bytes 32792
  4.7 42.9 %shard_map.84 = (bf16[128,512]{1,0:T(8,128)(2,1)S(1)}, f32[4,64,128]{2,1,0:T(8,128)S(1)}, f32[4,64,128]{2,1,0:T(8,128)S(1)}, f32[8,128]{1,0:T(8,128)S(1)}) custom-call(bf16[128,512]{1,0:T(8,128)(2,1)S(1)} %copy-done, bf16[128,128]{1,0:T(8,128)(2,1)S(1)} %copy-done.3, bf16[128,128]{1,0:T(8,128)(2,1)S(1)} %copy-done.4, bf16[4,64,128]{2,1,0:T(8,128)(2,1)S(1)} %bitcast.7, ...), custom_call_target="tpu_custom_call" | custom-call | tf_op jit(solution)/shard_map/pallas_call | solution.py:386
  47.6 0.5 %slice.3 = f32[1,1]{1,0:T(1,128)} slice(f32[8,128]{1,0:T(8,128)S(1)} %get-tuple-element.11), slice={[0:1], [0:1]} | slice | bytes 8 | tf_op jit(solution)/shard_map/slice | solution.py:447
  48.1 0.7 %copy.12 = bf16[128,512]{1,0:T(8,128)(2,1)} copy(bf16[128,512]{1,0:T(8,128)(2,1)S(1)} %get-tuple-element.16) | data formatting | bytes 262144
  48.8 0.7 %copy.13 = f32[4,128,64]{1,2,0:T(8,128)} copy(f32[4,128,64]{1,2,0:T(8,128)S(1)} %bitcast.6) | data formatting | bytes 262144
  49.4 0.7 %copy.14 = f32[4,128,64]{1,2,0:T(8,128)} copy(f32[4,128,64]{1,2,0:T(8,128)S(1)} %bitcast.5) | data formatting | bytes 262144
Async XLA Ops:
  0.6 0.9 %copy-start = (bf16[128,512]{1,0:T(8,128)(2,1)S(1)}, bf16[128,512]{1,0:T(8,128)(2,1)}, u32[]{:S(2)}) copy-start(bf16[128,512]{1,0:T(8,128)(2,1)} %q_ref.1) | copy-start | bytes 393220
  1.5 0.8 %copy-start.1 = (bf16[4,128,64]{1,2,0:T(8,128)(2,1)S(1)}, bf16[4,128,64]{1,2,0:T(8,128)(2,1)}, u32[]{:S(2)}) copy-start(bf16[4,128,64]{1,2,0:T(8,128)(2,1)} %param.8) | copy-start | bytes 196612
  2.4 0.8 %copy-start.2 = (bf16[4,128,64]{1,2,0:T(8,128)(2,1)S(1)}, bf16[4,128,64]{1,2,0:T(8,128)(2,1)}, u32[]{:S(2)}) copy-start(bf16[4,128,64]{1,2,0:T(8,128)(2,1)} %param.9) | copy-start | bytes 196612
  3.2 0.8 %copy-start.3 = (bf16[128,128]{1,0:T(8,128)(2,1)S(1)}, bf16[128,128]{1,0:T(8,128)(2,1)}, u32[]{:S(2)}) copy-start(bf16[128,128]{1,0:T(8,128)(2,1)} %k_ref.1) | copy-start | bytes 98308
  4.0 0.8 %copy-start.4 = (bf16[128,128]{1,0:T(8,128)(2,1)S(1)}, bf16[128,128]{1,0:T(8,128)(2,1)}, u32[]{:S(2)}) copy-start(bf16[128,128]{1,0:T(8,128)(2,1)} %v_ref.1) | copy-start | bytes 98308

commit v5 on v4

--- a/solution.py
+++ b/solution.py
@@ -441,7 +441,7 @@
             dma((heads_axis,)),
         ],
         compiler_params=pltpu.CompilerParams(
-            collective_id=0, has_side_effects=True, vmem_limit_bytes=40 * 1024 * 1024
+            collective_id=0, has_side_effects=True
         ),
     )(queries, keys, values, feat_q.swapaxes(1, 2), feat_k.swapaxes(1, 2))
     return student, grad_q.swapaxes(1, 2), grad_k.swapaxes(1, 2), error[0, 0]

time: 50.5 us -> 49.9 us (0.988)
  local copies, waits for them, and re-layouts: 6.57 us -> 4.41 us
  Pallas kernels: 42.9 us -> 44.6 us
    unnamed x13 -> x7, local copies, waits for them, and re-layouts: 6.05 us -> 3.21 us
    pallas_call x1, Pallas kernels: 42.9 us -> 44.6 us  [on_device(): pl.pallas_call(functools.partial(kernel, dims), out_shape=(jax.ShapeDtype...]
    slice x1, local copies, waits for them, and re-layouts: 0.51 us -> 1.2 us  [on_device(): return (student, grad_q.swapaxes(1, 2), grad_k.swapaxes(1, 2), error[0, 0])]
where the time goes in v5:
time: 49.9 us; the launch traced here: 49.7 us
  Pallas kernels  44.6 us (89%)
  local copies, waits for them, and re-layouts  4.41 us (9%)
  between operations  0.64 us (1%)
    pallas_call x1, Pallas kernels, on_device(): pl.pallas_call(functools.partial(kernel, dims), out_shape=(jax.ShapeDtype...  44.6 us
    unnamed x7, local copies, waits for them, and re-layouts  3.21 us
    slice x1, local copies, waits for them, and re-layouts, on_device(): return (student, grad_q.swapaxes(1, 2), grad_k.swapaxes(1, 2), error[0, 0])  1.2 us

profile of v5, /device:TPU:0, one launch (start us, length us, event | category | flops | bytes accessed | tf_op | source)
XLA Modules:
  0.0 49.7 jit_solution(3855050824662972559)
XLA Ops:
  0.6 44.6 %shard_map.84 = (bf16[128,512]{1,0:T(8,128)(2,1)}, f32[4,64,128]{2,1,0:T(8,128)}, f32[4,64,128]{2,1,0:T(8,128)}, f32[8,128]{1,0:T(8,128)}) custom-call(bf16[128,512]{1,0:T(8,128)(2,1)} %q_ref.1, bf16[128,128]{1,0:T(8,128)(2,1)} %k_ref.1, bf16[128,128]{1,0:T(8,128)(2,1)} %v_ref.1, bf16[4,64,128]{2,1,0:T(8,128)(2,1)} %bitcast.7, bf16[4,64,128]{2,1,0:T(8,128)(2,1)} %bitcast.8), custom_call_target="tpu_custom_call" | custom-call | tf_op jit(solution)/shard_map/pallas_call | solution.py:386
  45.3 1.2 %slice.3 = f32[1,1]{1,0:T(1,128)} slice(f32[8,128]{1,0:T(8,128)} %get-tuple-element.11), slice={[0:1], [0:1]} | slice | bytes 8 | tf_op jit(solution)/shard_map/slice | solution.py:447
  46.5 0.0 copy-start.1
  46.5 1.6 %copy.12 = bf16[128,512]{1,0:T(8,128)(2,1)} copy(bf16[128,512]{1,0:T(8,128)(2,1)} %get-tuple-element.16) | data formatting | bytes 262144
  48.1 0.0 copy-done.1
  48.1 0.0 copy-start
  48.1 0.7 %copy.13 = f32[4,128,64]{1,2,0:T(8,128)} copy(f32[4,128,64]{1,2,0:T(8,128)S(1)} %bitcast.6) | data formatting | bytes 262144
  48.7 0.3 copy-done
  49.0 0.7 %copy.14 = f32[4,128,64]{1,2,0:T(8,128)} copy(f32[4,128,64]{1,2,0:T(8,128)S(1)} %bitcast.5) | data formatting | bytes 262144
Async XLA Ops:
  46.5 1.6 %copy-start.1 = (f32[4,64,128]{2,1,0:T(8,128)S(1)}, f32[4,64,128]{2,1,0:T(8,128)}, u32[]{:S(2)}) copy-start(f32[4,64,128]{2,1,0:T(8,128)} %get-tuple-element.9) | copy-start | bytes 393220
  48.1 1.0 %copy-start = (f32[4,64,128]{2,1,0:T(8,128)S(1)}, f32[4,64,128]{2,1,0:T(8,128)}, u32[]{:S(2)}) copy-start(f32[4,64,128]{2,1,0:T(8,128)} %get-tuple-element.10) | copy-start | bytes 393220
